TPU v7x, 512 devices: a whole 4x4x16 slice. The times are simulated.
512 devices in a mesh: dp: 128 (over z, y, core), mp: 4 (over x).
Axes of the slice: x: 4, y: 4, z: 16, core: 2. Of those that a mesh axis runs over, the one named last changes fastest.
Arguments:
- queries: bfloat16 [24576, 4096], P('dp', 'mp'), as said below
- passages: bfloat16 [8192, 4096], P('dp', 'mp'), as said below
- pair_block: int32 [128, 128], P(None, 'dp'), may hold values from 0 to 3
- positives: int32 [24576], P('dp'), may hold values from 0 to 2047
Outputs:
- loss: float32 [], replicated
- query_grad: float32 [24576, 4096], P('dp', 'mp')
- passage_grad: float32 [8192, 4096], P('dp', 'mp')
Inputs may be any that keep to these rules, and one draw needn't show every extreme that they name: `queries`: query embeddings. `passages`: passage embeddings.
All inputs are finite; a program needn't handle non-finite values.
Results may differ from a plain program's by a relative error of at most 0.0019.
Values may be sent and summed in bfloat16 or wider, within the bound.
No kernel may reach another device: no remote copies, remote signals or barrier semaphores. Data moves between devices by JAX's collectives and lax.ppermute only.
A program may use at most 64 MiB of HBM per device.

v0:
```python
import jax
import jax.numpy as jnp
from jax import lax
from jax.sharding import PartitionSpec as P

PBLK = 16
PB_DEV = 4


def weigh(scores, picks):
    top = jnp.max(scores, axis=1, keepdims=True)
    shifted = jnp.exp(scores - top)
    total = jnp.sum(shifted, axis=1, keepdims=True)
    probs = shifted / total
    hits = picks[:, None] == lax.broadcasted_iota(jnp.int32, scores.shape, 1)
    chosen = jnp.sum(jnp.where(hits, scores, 0.0), axis=1)
    losses = top[:, 0] + jnp.log(total[:, 0]) - chosen
    weights = (probs - hits.astype(jnp.float32)).astype(jnp.bfloat16)
    return (weights, jnp.sum(losses))


def per_device(queries, passages, pair_block, positives):
    width = queries.shape[1]
    groups = lax.axis_size("dp")
    owned = passages.reshape(PB_DEV, PBLK, width)
    picked = pair_block[:, 0]
    outgoing = owned[picked]
    incoming = lax.all_to_all(outgoing, "dp", split_axis=0, concat_axis=0, tiled=True)
    flat = incoming.reshape(groups * PBLK, width)
    partial_value = lax.dot_general(
        queries, flat, (((1,), (1,)), ((), ())), preferred_element_type=jnp.float32
    )
    scores = lax.psum(partial_value, "mp")
    weights, loss_sum = weigh(scores, positives)
    loss = lax.psum(loss_sum, "dp") / (queries.shape[0] * groups)
    query_grad = jnp.dot(weights, flat, preferred_element_type=jnp.float32)
    cand_grad = lax.dot_general(
        weights, queries, (((0,), (0,)), ((), ())), preferred_element_type=jnp.float32
    )
    returned = lax.all_to_all(
        cand_grad.reshape(groups, PBLK, width), "dp", split_axis=0, concat_axis=0, tiled=True
    )
    onehot = (picked[:, None] == jnp.arange(PB_DEV, dtype=jnp.int32)[None, :]).astype(jnp.float32)
    summed = jnp.einsum("jk,jrd->krd", onehot, returned, precision=lax.Precision.HIGHEST)
    passage_grad = summed.reshape(PB_DEV * PBLK, width)
    return (loss, query_grad, passage_grad)


def solution(mesh):
    in_specs = (P("dp", "mp"), P("dp", "mp"), P(None, "dp"), P("dp"))
    out_specs = (P(), P("dp", "mp"), P("dp", "mp"))
    return jax.shard_map(
        per_device, mesh=mesh, in_specs=in_specs, out_specs=out_specs, check_vma=False
    )
```

profile of v0, /device:TPU:1, one launch (start us, length us, event | category | flops | bytes accessed | tf_op | source)
XLA Modules:
  0.0 935.9 jit_solution(9183723598633380238)
XLA Ops:
  7.2 0.0 copy-start
  7.2 0.0 all-reduce.2.cloned.1.call-start
  7.2 0.7 fusion.6
  7.9 3.6 gather_fusion
  11.6 204.4 %all_to_all.10 = bf16[128,16,1024]{2,1,0:T(8,128)(2,1)S(1)} all-to-all(bf16[128,16,1024]{2,1,0:T(8,128)(2,1)} %gather_fusion), channel_id=1, replica_groups=mesh['dp'=128,'mp'=4] {'dp'}, dimensions={0} | all-to-all | bytes 8388608 | tf_op jit(solution)/shard_map/all_to_all | solution.py:28
  216.0 1.9 copy-done.2
  217.9 0.0 copy-done
  217.9 2.7 convolution_bitcast_fusion
  220.6 0.0 all-reduce.2.cloned.1.call-update
  220.7 63.7 %all-reduce.2.cloned.1.call-done = f32[192,2048]{1,0:T(8,128)} async-done(((f32[192,2048]{1,0:T(8,128)}), f32[192,2048]{1,0:T(8,128)}) %all-reduce.2.cloned.1.call-update) | async-done | bytes 1572880 | tf_op jit(solution)/shard_map/psum | solution.py:33
  284.4 1.7 reduce_max.9
  286.1 0.0 copy-done.3
  286.1 0.2 copy-done.1
  286.3 0.5 fusion.2
  286.8 4.7 fusion.7
  291.5 17.2 %all-to-all-start.1 = ((f32[128,16,1024]{2,1,0:T(8,128)}), f32[128,16,1024]{2,1,0:T(8,128)}, u32[]{:S(2)}, u32[]{:S(2)}) async-start(f32[128,16,1024]{2,1,0:T(8,128)} %bitcast.17), calls=%async_computation.1 | async-start | bytes 16777216 | tf_op jit(solution)/shard_map/all_to_all | solution.py:40
  308.7 0.6 subtract_reduce_fusion
  309.4 602.4 %psum.15 = f32[]{:T(128)} all-reduce(f32[]{:T(128)} %subtract_reduce_fusion), channel_id=1, replica_groups=mesh['dp'=128,'mp'=4] {'dp'}, use_global_device_ids=true, to_apply=%region_5.6 | all-reduce | flops 1 | bytes 8 | tf_op jit(solution)/shard_map/psum | solution.py:35
  912.4 0.0 copy-start.4
  912.4 4.2 fusion.8
  916.7 0.0 all-to-all-done.1
  916.7 0.0 copy-done.4
  916.7 10.4 %fusion = f32[4,16,1024]{2,0,1:T(4,128)S(1)} fusion(f32[128,16,1024]{2,1,0:T(8,128)} %all-to-all-done.1, s32[128]{0:T(128)S(1)} %bitcast.21), kind=kOutput, calls=%fused_computation.1 | convolution fusion | flops 100663808 | bytes 8651264 | tf_op jit(solution)/shard_map/jk,jrd->krd/dot_general | solution.py:44
  927.1 0.9 copy.11
  (4 shorter events, 0.0 us)
Async XLA Ops:
  7.2 210.8 %copy-start = (bf16[192,1024]{1,0:T(8,128)(2,1)S(1)}, bf16[192,1024]{1,0:T(8,128)(2,1)}, u32[]{:S(2)}) copy-start(bf16[192,1024]{1,0:T(8,128)(2,1)} %param.4) | copy-start | bytes 1179652
  7.2 277.2 %all-reduce.2.cloned.1.call-start = ((), (), s32[]{:S(2)}) async-start(), calls=%async_computation.2 | async-start | bytes 3145728 | tf_op jit(solution)/shard_map/psum | solution.py:33
  216.0 1.9 copy-start.2
  220.6 65.5 %copy-start.3 = (s32[192]{0:T(256)S(1)}, s32[192]{0:T(256)}, u32[]{:S(2)}) copy-start(s32[192]{0:T(256)} %param.7) | copy-start | bytes 2308
  284.4 1.9 copy-start.1
  291.5 625.2 %all-to-all-start.1 = ((f32[128,16,1024]{2,1,0:T(8,128)}), f32[128,16,1024]{2,1,0:T(8,128)}, u32[]{:S(2)}, u32[]{:S(2)}) async-start(f32[128,16,1024]{2,1,0:T(8,128)} %bitcast.17), calls=%async_computation.1 | async-start | bytes 16777216 | tf_op jit(solution)/shard_map/all_to_all | solution.py:40
  912.4 4.2 copy-start.4
Sparse Core Ops, SparseCore 0:
  220.8 63.5 all-reduce.1
where the time goes:
time: 936 us
  blocking collectives  807 us (86%)
  waiting for transfers between devices  63.8 us (7%)
  matrix products  22 us (2%)
  starting transfers between devices  17.3 us (2%)
  between operations  15.8 us (2%)
    psum x1, blocking collectives, per_device(): loss = lax.psum(loss_sum, 'dp') / (queries.shape[0] * groups)  602 us
    all_to_all x1, blocking collectives, per_device(): lax.all_to_all(outgoing, 'dp', split_axis=0, concat_axis=0, tiled=True)  204 us
    psum x1, waiting for transfers between devices, per_device(): scores = lax.psum(partial_value, 'mp')  63.7 us
  transfers between devices with their start and end apart: 2, of which 1 were waited for; matrix products, arithmetic and copies ran while one was open for 1% of the time, Pallas kernels for 0%

commit v1 on v0

v1 whole, which is shorter than its diff:
```python
import jax
import jax.numpy as jnp
from jax import lax
from jax.experimental import pallas as pl
from jax.experimental.pallas import tpu as pltpu
from jax.sharding import Mesh, PartitionSpec as P

NZ, NY, NC, NX = 16, 4, 2, 4
NB = NY * NC
QBLK = 192
PBLK = 16
PB_DEV = 4
GROUP = PBLK * PB_DEV
QUERIES = NZ * NB * QBLK
CAND = NZ * PBLK
SHARE = QBLK // NX
DP = ("z", "y", "core")
ROW = ("y", "core", "x")


def pick_rows(sel_ref, p_ref, chosen, b):
    for z in range(NZ):
        start = pl.multiple_of(z * GROUP + sel_ref[z * NB + b] * PBLK, PBLK)
        chosen[z * PBLK : (z + 1) * PBLK, :] = p_ref[pl.ds(start, PBLK), :]


def scores_kernel(sel_ref, tab_ref, q_ref, p_ref, s_ref, chosen):
    pick_rows(sel_ref, p_ref, chosen, pl.program_id(0))
    s_ref[...] = lax.dot_general(
        q_ref[0], chosen[...], (((1,), (1,)), ((), ())), preferred_element_type=jnp.float32
    )


def partial_scores(sel, tab, q_all, p_all):
    width = q_all.shape[2]
    return pl.pallas_call(
        scores_kernel,
        out_shape=jax.ShapeDtypeStruct((NB * QBLK, CAND), jnp.float32),
        grid_spec=pltpu.PrefetchScalarGridSpec(
            num_scalar_prefetch=2,
            grid=(NB,),
            in_specs=[
                pl.BlockSpec((1, QBLK, width), lambda b, sel, tab: (tab[b], 0, 0)),
                pl.BlockSpec((NZ * GROUP, width), lambda b, sel, tab: (0, 0)),
            ],
            out_specs=pl.BlockSpec((QBLK, CAND), lambda b, sel, tab: (b, 0)),
            scratch_shapes=[pltpu.VMEM((CAND, width), jnp.bfloat16)],
        ),
        compiler_params=pltpu.CompilerParams(vmem_limit_bytes=40 << 20),
        cost_estimate=pl.CostEstimate(
            flops=2 * NB * QBLK * CAND * width,
            bytes_accessed=2 * (NB * QBLK + NZ * GROUP) * width + 4 * NB * QBLK * CAND,
            transcendentals=0,
        ),
        name="partial_scores",
    )(sel, tab, q_all, p_all)


def weigh_kernel(s_ref, pos_ref, w_ref, loss_ref, total):
    for j in range(NB):
        total[j] = (s_ref[j, 0] + s_ref[j, 1]) + (s_ref[j, 2] + s_ref[j, 3])
    scores = total[...]
    top = jnp.max(jnp.max(scores, axis=0), axis=1, keepdims=True)
    shifted = jnp.exp(scores - top[None])
    denom = jnp.sum(jnp.sum(shifted, axis=0), axis=1, keepdims=True)
    probs = shifted / denom[None]
    lane = lax.broadcasted_iota(jnp.int32, scores.shape, 2)
    col = lax.broadcasted_iota(jnp.int32, scores.shape, 0)
    index = ((lane // PBLK) * NB + col) * PBLK + lane % PBLK
    hits = index == pos_ref[...][None]
    chosen = jnp.sum(jnp.sum(jnp.where(hits, scores, 0.0), axis=0), axis=1, keepdims=True)
    weights = (probs - hits.astype(jnp.float32)).astype(jnp.bfloat16)
    for x in range(NX):
        w_ref[:, x] = weights
    loss = jnp.sum(top + jnp.log(denom) - chosen, axis=0, keepdims=True)
    loss_ref[...] = jnp.broadcast_to(loss, loss_ref.shape)


def weigh(parts, picks):
    return pl.pallas_call(
        weigh_kernel,
        out_shape=(
            jax.ShapeDtypeStruct((NB, NX, SHARE, CAND), jnp.bfloat16),
            jax.ShapeDtypeStruct((8, 128), jnp.float32),
        ),
        scratch_shapes=[pltpu.VMEM((NB, SHARE, CAND), jnp.float32)],
        compiler_params=pltpu.CompilerParams(vmem_limit_bytes=40 << 20),
        cost_estimate=pl.CostEstimate(
            flops=20 * NB * SHARE * CAND, bytes_accessed=6 * NB * NX * SHARE * CAND, transcendentals=NB * SHARE * CAND
        ),
        name="weigh",
    )(parts, picks)


def grads_kernel(sel_ref, tab_ref, out_ref, q_ref, p_ref, w_ref, qg_ref, pg_ref, chosen):
    b = pl.program_id(0)

    @pl.when(b == 0)
    def _():
        pg_ref[...] = jnp.zeros_like(pg_ref)

    pick_rows(sel_ref, p_ref, chosen, b)
    weights = w_ref[...]
    qg_ref[0] = jnp.dot(weights, chosen[...], preferred_element_type=jnp.float32)
    cand = lax.dot_general(
        weights, q_ref[0], (((0,), (0,)), ((), ())), preferred_element_type=jnp.float32
    )
    for z in range(NZ):
        start = pl.multiple_of(z * GROUP + sel_ref[z * NB + b] * PBLK, PBLK)
        pg_ref[pl.ds(start, PBLK), :] += cand[z * PBLK : (z + 1) * PBLK, :]


def grads(sel, tab, out, q_all, p_all, weights):
    width = q_all.shape[2]
    return pl.pallas_call(
        grads_kernel,
        out_shape=(
            jax.ShapeDtypeStruct((NB, QBLK, width), jnp.float32),
            jax.ShapeDtypeStruct((NZ * GROUP, width), jnp.float32),
        ),
        grid_spec=pltpu.PrefetchScalarGridSpec(
            num_scalar_prefetch=3,
            grid=(NB,),
            in_specs=[
                pl.BlockSpec((1, QBLK, width), lambda b, sel, tab, out: (tab[b], 0, 0)),
                pl.BlockSpec((NZ * GROUP, width), lambda b, sel, tab, out: (0, 0)),
                pl.BlockSpec((QBLK, CAND), lambda b, sel, tab, out: (b, 0)),
            ],
            out_specs=(
                pl.BlockSpec((1, QBLK, width), lambda b, sel, tab, out: (out[b], 0, 0)),
                pl.BlockSpec((NZ * GROUP, width), lambda b, sel, tab, out: (0, 0)),
            ),
            scratch_shapes=[pltpu.VMEM((CAND, width), jnp.bfloat16)],
        ),
        compiler_params=pltpu.CompilerParams(vmem_limit_bytes=40 << 20),
        cost_estimate=pl.CostEstimate(
            flops=4 * NB * QBLK * CAND * width,
            bytes_accessed=(6 * NB * QBLK + 6 * NZ * GROUP) * width + 2 * NB * QBLK * CAND,
            transcendentals=0,
        ),
        name="grads",
    )(sel, tab, out, q_all, p_all, weights)


def total_over(value, axis, size):
    copies = jnp.broadcast_to(value[None], (size,) + value.shape)
    return jnp.sum(lax.all_to_all(copies, axis, split_axis=0, concat_axis=0, tiled=True), axis=0)


def per_device(queries, passages, pair_block, positives):
    y, core, x = lax.axis_index("y"), lax.axis_index("core"), lax.axis_index("x")
    p_all = lax.all_gather(passages, "z", axis=0, tiled=True)
    sel = lax.all_to_all(
        pair_block.reshape(NZ, NB), "z", split_axis=0, concat_axis=0, tiled=True
    ).reshape(NZ * NB)
    parts = [queries]
    for k in range(1, NY):
        parts.append(lax.ppermute(queries, "y", [(i, (i + k) % NY) for i in range(NY)]))
    mine = jnp.stack(parts)
    other = lax.ppermute(mine, "core", [(0, 1), (1, 0)])
    q_all = jnp.concatenate([mine, other], axis=0)
    block = jnp.arange(NB, dtype=jnp.int32)
    block_y, away = block // NC, ((block % NC) != core).astype(jnp.int32)
    tab = away * NY + (y - block_y + NY) % NY
    out = away * NY + block_y

    part = partial_scores(sel, tab, q_all, p_all)
    swapped = lax.all_to_all(
        part.reshape(NB * NX, SHARE, CAND), ROW, split_axis=0, concat_axis=0, tiled=True
    )
    picks = lax.dynamic_slice(positives, (x * SHARE,), (SHARE,)).reshape(SHARE, 1)
    weights, loss = weigh(swapped.reshape(NB, NX, SHARE, CAND), picks)
    weights = lax.all_to_all(
        weights.reshape(NB * NX, SHARE, CAND), ROW, split_axis=0, concat_axis=0, tiled=True
    ).reshape(NB * QBLK, CAND)
    query_part, passage_part = grads(sel, tab, out, q_all, p_all, weights)

    passage_grad = lax.psum_scatter(passage_part, "z", scatter_dimension=0, tiled=True)
    arrived = lax.ppermute(query_part[NY:], "core", [(0, 1), (1, 0)])
    query_grad = jnp.sum(
        lax.all_to_all(query_part[:NY] + arrived, "y", split_axis=0, concat_axis=0, tiled=True),
        axis=0,
    )
    loss = total_over(total_over(loss, ROW, NB * NX), "z", NZ)[0, 0] / QUERIES
    return loss, query_grad, passage_grad


def solution(mesh):
    fine = Mesh(mesh.devices.reshape(NZ, NY, NC, NX), DP + ("x",))
    in_specs = (P(DP, "x"), P(DP, "x"), P(None, DP), P(DP))
    out_specs = (P(), P(DP, "x"), P(DP, "x"))
    return jax.shard_map(
        per_device, mesh=fine, in_specs=in_specs, out_specs=out_specs, check_vma=False
    )
```

time: 936 us -> 244 us (0.26)
  the two profiles are of different devices: /device:TPU:1 before, /device:TPU:2 now
where the time goes in v1:
time: 244 us; the launch traced here: 243 us
  waiting for transfers between devices  117 us (48%)
  starting transfers between devices  56.3 us (23%)
  local copies, waits for them, and re-layouts  16.6 us (7%)
  between operations  16.1 us (7%)
  Pallas kernels  13.3 us (5%)
  blocking collectives  12 us (5%)
  other arithmetic  11.3 us (5%)
    all_to_all x1, waiting for transfers between devices, per_device(): lax.all_to_all(query_part[:NY] + arrived, 'y', split_axis=0, concat_axis=...  34.8 us
    all_to_all x1, waiting for transfers between devices, per_device(): lax.all_to_all(part.reshape(NB * NX, SHARE, CAND), ROW, split_axis=0, con...  20.4 us
    all_gather x1, waiting for transfers between devices, per_device(): p_all = lax.all_gather(passages, 'z', axis=0, tiled=True)  16.1 us
    all_to_all x1, starting transfers between devices, per_device(): lax.all_to_all(pair_block.reshape(NZ, NB), 'z', split_axis=0, concat_axis...  15.2 us
    ppermute x3, waiting for transfers between devices, per_device(): lax.ppermute(queries, 'y', [(i, (i + k) % NY) for i in range(NY)])  12.9 us
    all_to_all x1, waiting for transfers between devices, per_device(): lax.all_to_all(pair_block.reshape(NZ, NB), 'z', split_axis=0, concat_axis...  12.1 us
    all_to_all x1, waiting for transfers between devices, per_device(): lax.all_to_all(weights.reshape(NB * NX, SHARE, CAND), ROW, split_axis=0,...  12.1 us
    all_to_all x1, blocking collectives, total_over(): lax.all_to_all(copies, axis, split_axis=0, concat_axis=0, tiled=True)  12 us
  transfers between devices with their start and end apart: 12, of which 9 were waited for; matrix products, arithmetic and copies ran while one was open for 8% of the time, Pallas kernels for 0%

profile of v1, /device:TPU:2, one launch (start us, length us, event | category | flops | bytes accessed | tf_op | source)
XLA Modules:
  0.0 243.0 jit_solution(11107550266203135064)
XLA Ops:
  7.9 3.5 %collective-permute-start = (bf16[192,1024]{1,0:T(8,128)(2,1)}, bf16[192,1024]{1,0:T(8,128)(2,1)S(1)}, u32[]{:S(2)}, u32[]{:S(2)}) collective-permute-start(bf16[192,1024]{1,0:T(8,128)(2,1)} %param.4), channel_id=1, source_target_pairs={{0,8},{8,16},{16,24},{24,0},{1,9},{9,17},{17,25},{25,1},{2,10},{10... | collective-permute-start | bytes 1179656 | tf_op jit(solution)/shard_map/ppermute | solution.py:158
  11.4 3.6 %collective-permute-start.2 = (bf16[192,1024]{1,0:T(8,128)(2,1)}, bf16[192,1024]{1,0:T(8,128)(2,1)S(1)}, u32[]{:S(2)}, u32[]{:S(2)}) collective-permute-start(bf16[192,1024]{1,0:T(8,128)(2,1)} %param.4), channel_id=1, source_target_pairs={{0,24},{8,0},{16,8},{24,16},{1,25},{9,1},{17,9},{25,17},{2,26},{10... | collective-permute-start | bytes 1179656 | tf_op jit(solution)/shard_map/ppermute | solution.py:158
  15.0 3.9 %collective-permute-start.1 = (bf16[192,1024]{1,0:T(8,128)(2,1)}, bf16[192,1024]{1,0:T(8,128)(2,1)S(1)}, u32[]{:S(2)}, u32[]{:S(2)}) collective-permute-start(bf16[192,1024]{1,0:T(8,128)(2,1)} %param.4), channel_id=1, source_target_pairs={{0,16},{8,24},{16,0},{24,8},{1,17},{9,25},{17,1},{25,9},{2,18},{10... | collective-permute-start | bytes 1179656 | tf_op jit(solution)/shard_map/ppermute | solution.py:158
  18.9 3.3 %collective-permute-done = bf16[192,1024]{1,0:T(8,128)(2,1)S(1)} collective-permute-done((bf16[192,1024]{1,0:T(8,128)(2,1)}, bf16[192,1024]{1,0:T(8,128)(2,1)S(1)}, u32[]{:S(2)}, u32[]{:S(2)}) %collective-permute-start) | collective-permute-done | bytes 393248 | tf_op jit(solution)/shard_map/ppermute | solution.py:158
  22.2 3.4 %collective-permute-done.2 = bf16[192,1024]{1,0:T(8,128)(2,1)S(1)} collective-permute-done((bf16[192,1024]{1,0:T(8,128)(2,1)}, bf16[192,1024]{1,0:T(8,128)(2,1)S(1)}, u32[]{:S(2)}, u32[]{:S(2)}) %collective-permute-start.2) | collective-permute-done | bytes 393248 | tf_op jit(solution)/shard_map/ppermute | solution.py:158
  25.6 6.2 %collective-permute-done.1 = bf16[192,1024]{1,0:T(8,128)(2,1)S(1)} collective-permute-done((bf16[192,1024]{1,0:T(8,128)(2,1)}, bf16[192,1024]{1,0:T(8,128)(2,1)S(1)}, u32[]{:S(2)}, u32[]{:S(2)}) %collective-permute-start.1) | collective-permute-done | bytes 393248 | tf_op jit(solution)/shard_map/ppermute | solution.py:158
  31.8 2.5 %pad_maximum_fusion = bf16[4,192,1024]{2,1,0:T(8,128)(2,1)} fusion(bf16[1,192,1024]{2,1,0:T(8,128)(2,1)S(1)} %bitcast.20, bf16[1,192,1024]{2,1,0:T(8,128)(2,1)S(1)} %bitcast.22, bf16[1,192,1024]{2,1,0:T(8,128)(2,1)S(1)} %bitcast.21, bf16[1,192,1024]{2,1,0:T(8,128)(2,1)} %bitcast.19), kind=kLoop, calls=%fused_computation.1 | loop fusion | flops 2359296 | bytes 3145728 | tf_op jit(solution)/shard_map/stack | solution.py:159
  38.1 15.2 %all-to-all-start = ((s32[16,1,8]{2,1,0:T(1,128)}), s32[16,1,8]{2,1,0:T(1,128)}, u32[]{:S(2)}, u32[]{:S(2)}) async-start(s32[16,1,8]{2,1,0:T(1,128)} %bitcast), calls=%async_computation | async-start | bytes 16384 | tf_op jit(solution)/shard_map/all_to_all | solution.py:153
  53.4 12.1 %all-to-all-done = s32[16,1,8]{2,1,0:T(1,128)} async-done(((s32[16,1,8]{2,1,0:T(1,128)}), s32[16,1,8]{2,1,0:T(1,128)}, u32[]{:S(2)}, u32[]{:S(2)}) %all-to-all-start) | async-done | bytes 544 | tf_op jit(solution)/shard_map/all_to_all | solution.py:153
  71.6 16.1 %all-gather.2.cloned.1.call-done.p_ref = bf16[1024,1024]{1,0:T(8,128)(2,1)} async-done(((bf16[64,1024]{1,0:T(8,128)(2,1)}), bf16[1024,1024]{1,0:T(8,128)(2,1)}) %all-gather.2.cloned.1.call-update) | async-done | bytes 2097168 | tf_op jit(solution)/shard_map/all_gather | solution.py:152
  89.3 3.2 %partial_scores.1 = f32[1536,256]{1,0:T(8,128)S(1)} custom-call(s32[128]{0:T(128)S(1)} %reshape.33.sel_ref, s32[8]{0:T(128)S(1)} %fusion.tab_ref, bf16[8,192,1024]{2,1,0:T(8,128)(2,1)S(1)} %constant_dynamic-update-slice_fusion.q_ref, bf16[1024,1024]{1,0:T(8,128)(2,1)S(1)} %copy-done.1), custom_call_target="tpu_custom_call" | custom-call | flops 805306368 | bytes 6815744 | tf_op jit(solution)/shard_map/partial_scores/pallas_call | solution.py:36
  93.7 7.5 %all-to-all-start.1 = ((f32[32,48,256]{2,1,0:T(8,128)}), f32[32,48,256]{2,1,0:T(8,128)}, u32[]{:S(2)}, u32[]{:S(2)}) async-start(f32[32,48,256]{2,1,0:T(8,128)} %bitcast.17), calls=%async_computation.1 | async-start | bytes 3145728 | tf_op jit(solution)/shard_map/all_to_all | solution.py:168
  101.4 20.4 %all-to-all-done.1 = f32[32,48,256]{2,1,0:T(8,128)} async-done(((f32[32,48,256]{2,1,0:T(8,128)}), f32[32,48,256]{2,1,0:T(8,128)}, u32[]{:S(2)}, u32[]{:S(2)}) %all-to-all-start.1) | async-done | bytes 1572896 | tf_op jit(solution)/shard_map/all_to_all | solution.py:168
  124.4 6.5 %all-to-all-start.4 = ((bf16[32,48,256]{2,1,0:T(8,128)(2,1)}), bf16[32,48,256]{2,1,0:T(8,128)(2,1)}, u32[]{:S(2)}, u32[]{:S(2)}) async-start(bf16[32,48,256]{2,1,0:T(8,128)(2,1)} %bitcast.18), calls=%async_computation.4 | async-start | bytes 1572864 | tf_op jit(solution)/shard_map/all_to_all | solution.py:173
  130.9 12.1 %all-to-all-done.4 = bf16[32,48,256]{2,1,0:T(8,128)(2,1)} async-done(((bf16[32,48,256]{2,1,0:T(8,128)(2,1)}), bf16[32,48,256]{2,1,0:T(8,128)(2,1)}, u32[]{:S(2)}, u32[]{:S(2)}) %all-to-all-start.4) | async-done | bytes 786464 | tf_op jit(solution)/shard_map/all_to_all | solution.py:173
  144.6 8.3 %grads.1 = (f32[8,192,1024]{2,1,0:T(8,128)}, f32[1024,1024]{1,0:T(8,128)S(1)}) custom-call(s32[128]{0:T(128)S(1)} %reshape.33.sel_ref, s32[8]{0:T(128)S(1)} %fusion.tab_ref, s32[8]{0:T(128)S(1)} %fusion.2.out_ref, bf16[8,192,1024]{2,1,0:T(8,128)(2,1)S(1)} %constant_dynamic-update-slice_fusion.q_ref, bf16[1024,1024]{1,0:T(8,128)(2,1)S(1)} %copy-done.2, ...), custom_call_target="tpu_custom_call" | custom-call | flops 1610612736 | bytes 16515072 | tf_op jit(solution)/shard_map/grads/pallas_call | solution.py:115
  155.0 2.1 slice.11
  157.1 2.7 %collective-permute-start.4 = (f32[4,192,1024]{2,1,0:T(8,128)S(1)}, f32[4,192,1024]{2,1,0:T(8,128)}, u32[]{:S(2)}, u32[]{:S(2)}) collective-permute-start(f32[4,192,1024]{2,1,0:T(8,128)S(1)} %slice.11), channel_id=1, source_target_pairs={{0,4},{4,0},{1,5},{5,1},{2,6},{6,2},{3,7},{7,3},{8,12},{12,8},{9,1... | collective-permute-start | bytes 9437192 | tf_op jit(solution)/shard_map/ppermute | solution.py:179
  159.8 12.0 %all_to_all.34 = f32[32,8,128]{2,1,0:T(8,128)S(1)} all-to-all(f32[32,8,128]{2,1,0:T(8,128)S(1)} %broadcast_in_dim.4), channel_id=1, replica_groups=mesh['z'=16,'y'=4,'core'=2,'x'=4] {'y','core','x'}, dimensions={0} | all-to-all | bytes 262144 | tf_op jit(solution)/shard_map/all_to_all | solution.py:147
  172.5 7.7 %all-to-all-start.3 = ((f32[16,8,128]{2,1,0:T(8,128)}), f32[16,8,128]{2,1,0:T(8,128)S(1)}, u32[]{:S(2)}, u32[]{:S(2)}) async-start(f32[16,8,128]{2,1,0:T(8,128)} %broadcast_in_dim.5), calls=%async_computation.3 | async-start | bytes 131072 | tf_op jit(solution)/shard_map/all_to_all | solution.py:147
  180.3 5.5 %slice_add_fusion = f32[4,192,1024]{2,1,0:T(8,128)} fusion(f32[4,192,1024]{2,1,0:T(8,128)} %collective-permute-done.4, f32[8,192,1024]{2,1,0:T(8,128)} %get-tuple-element.9), kind=kLoop, calls=%fused_computation | loop fusion | flops 786432 | bytes 9437184 | tf_op jit(solution)/shard_map/add | solution.py:181
  185.7 8.3 %all-to-all-done.3 = f32[16,8,128]{2,1,0:T(8,128)S(1)} async-done(((f32[16,8,128]{2,1,0:T(8,128)}), f32[16,8,128]{2,1,0:T(8,128)S(1)}, u32[]{:S(2)}, u32[]{:S(2)}) %all-to-all-start.3) | async-done | bytes 65568 | tf_op jit(solution)/shard_map/all_to_all | solution.py:147
  194.1 3.7 %all-to-all-start.5 = ((f32[4,192,1024]{2,1,0:T(8,128)}), f32[4,192,1024]{2,1,0:T(8,128)S(1)}, u32[]{:S(2)}, u32[]{:S(2)}) async-start(f32[4,192,1024]{2,1,0:T(8,128)} %slice_add_fusion), calls=%async_computation.5 | async-start | bytes 6291456 | tf_op jit(solution)/shard_map/all_to_all | solution.py:181
  199.0 34.8 %all-to-all-done.5 = f32[4,192,1024]{2,1,0:T(8,128)S(1)} async-done(((f32[4,192,1024]{2,1,0:T(8,128)}), f32[4,192,1024]{2,1,0:T(8,128)S(1)}, u32[]{:S(2)}, u32[]{:S(2)}) %all-to-all-start.5) | async-done | bytes 3145760 | tf_op jit(solution)/shard_map/all_to_all | solution.py:181
  (51 shorter events, 22.3 us)
Async XLA Ops:
  7.2 94.1 %copy-start = (s32[192]{0:T(256)S(1)}, s32[192]{0:T(256)}, u32[]{:S(2)}) copy-start(s32[192]{0:T(256)} %param.7) | copy-start | bytes 2308
  7.2 46.2 %copy-start.6 = (bf16[192,1024]{1,0:T(8,128)(2,1)S(1)}, bf16[192,1024]{1,0:T(8,128)(2,1)}, u32[]{:S(2)}) copy-start(bf16[192,1024]{1,0:T(8,128)(2,1)} %param.4) | copy-start | bytes 1179652
  7.2 29.5 %copy-start.10 = (s32[128,1]{0,1:T(1,128)S(1)}, s32[128,1]{0,1:T(1,128)}, u32[]{:S(2)}) copy-start(s32[128,1]{0,1:T(1,128)} %param.6) | copy-start | bytes 1540
  7.2 80.5 %all-gather.2.cloned.1.call-start = ((), (), s32[]{:S(2)}) async-start(), calls=%async_computation.7 | async-start | bytes 2228224 | tf_op jit(solution)/shard_map/all_gather | solution.py:152
  7.9 14.2 %collective-permute-start = (bf16[192,1024]{1,0:T(8,128)(2,1)}, bf16[192,1024]{1,0:T(8,128)(2,1)S(1)}, u32[]{:S(2)}, u32[]{:S(2)}) collective-permute-start(bf16[192,1024]{1,0:T(8,128)(2,1)} %param.4), channel_id=1, source_target_pairs={{0,8},{8,16},{16,24},{24,0},{1,9},{9,17},{17,25},{25,1},{2,10},{10... | collective-permute-start | bytes 1179656 | tf_op jit(solution)/shard_map/ppermute | solution.py:158
  11.4 14.1 %collective-permute-start.2 = (bf16[192,1024]{1,0:T(8,128)(2,1)}, bf16[192,1024]{1,0:T(8,128)(2,1)S(1)}, u32[]{:S(2)}, u32[]{:S(2)}) collective-permute-start(bf16[192,1024]{1,0:T(8,128)(2,1)} %param.4), channel_id=1, source_target_pairs={{0,24},{8,0},{16,8},{24,16},{1,25},{9,1},{17,9},{25,17},{2,26},{10... | collective-permute-start | bytes 1179656 | tf_op jit(solution)/shard_map/ppermute | solution.py:158
  15.0 16.8 %collective-permute-start.1 = (bf16[192,1024]{1,0:T(8,128)(2,1)}, bf16[192,1024]{1,0:T(8,128)(2,1)S(1)}, u32[]{:S(2)}, u32[]{:S(2)}) collective-permute-start(bf16[192,1024]{1,0:T(8,128)(2,1)} %param.4), channel_id=1, source_target_pairs={{0,16},{8,24},{16,0},{24,8},{1,17},{9,25},{17,1},{25,9},{2,18},{10... | collective-permute-start | bytes 1179656 | tf_op jit(solution)/shard_map/ppermute | solution.py:158
  22.2 31.1 %copy-start.8 = (bf16[192,1024]{1,0:T(8,128)(2,1)}, bf16[192,1024]{1,0:T(8,128)(2,1)S(1)}, u32[]{:S(2)}) copy-start(bf16[192,1024]{1,0:T(8,128)(2,1)S(1)} %collective-permute-done) | copy-start | bytes 1179652
  25.6 27.8 %copy-start.7 = (bf16[192,1024]{1,0:T(8,128)(2,1)}, bf16[192,1024]{1,0:T(8,128)(2,1)S(1)}, u32[]{:S(2)}) copy-start(bf16[192,1024]{1,0:T(8,128)(2,1)S(1)} %collective-permute-done.2) | copy-start | bytes 1179652
  31.8 21.6 %copy-start.9 = (bf16[192,1024]{1,0:T(8,128)(2,1)}, bf16[192,1024]{1,0:T(8,128)(2,1)S(1)}, u32[]{:S(2)}) copy-start(bf16[192,1024]{1,0:T(8,128)(2,1)S(1)} %collective-permute-done.1) | copy-start | bytes 1179652
  34.3 35.8 %collective-permute-start.3 = (bf16[4,192,1024]{2,1,0:T(8,128)(2,1)}, bf16[4,192,1024]{2,1,0:T(8,128)(2,1)}, u32[]{:S(2)}, u32[]{:S(2)}) collective-permute-start(bf16[4,192,1024]{2,1,0:T(8,128)(2,1)} %pad_maximum_fusion), channel_id=1, source_target_pairs={{0,4},{4,0},{1,5},{5,1},{2,6},{6,2},{3,7},{7,3},{8,12},{12,8},{9,1... | collective-permute-start | bytes 4718600 | tf_op jit(solution)/shard_map/ppermute | solution.py:160
  38.1 27.5 %all-to-all-start = ((s32[16,1,8]{2,1,0:T(1,128)}), s32[16,1,8]{2,1,0:T(1,128)}, u32[]{:S(2)}, u32[]{:S(2)}) async-start(s32[16,1,8]{2,1,0:T(1,128)} %bitcast), calls=%async_computation | async-start | bytes 16384 | tf_op jit(solution)/shard_map/all_to_all | solution.py:153
  87.7 1.6 copy-start.1
  92.5 1.2 copy-start.3
  93.7 28.1 %all-to-all-start.1 = ((f32[32,48,256]{2,1,0:T(8,128)}), f32[32,48,256]{2,1,0:T(8,128)}, u32[]{:S(2)}, u32[]{:S(2)}) async-start(f32[32,48,256]{2,1,0:T(8,128)} %bitcast.17), calls=%async_computation.1 | async-start | bytes 3145728 | tf_op jit(solution)/shard_map/all_to_all | solution.py:168
  123.5 0.9 copy-start.5
  124.4 18.6 %all-to-all-start.4 = ((bf16[32,48,256]{2,1,0:T(8,128)(2,1)}), bf16[32,48,256]{2,1,0:T(8,128)(2,1)}, u32[]{:S(2)}, u32[]{:S(2)}) async-start(bf16[32,48,256]{2,1,0:T(8,128)(2,1)} %bitcast.18), calls=%async_computation.4 | async-start | bytes 1572864 | tf_op jit(solution)/shard_map/all_to_all | solution.py:173
  130.9 104.2 %reduce-scatter.2.cloned.1.call-start = ((), (), s32[]{:S(2)}) async-start(), calls=%async_computation.8 | async-start | bytes 4456448 | tf_op jit(solution)/shard_map/reduce_scatter | solution.py:178
  143.0 1.6 copy-start.2
  152.9 2.0 copy-start.4
  157.1 23.2 %collective-permute-start.4 = (f32[4,192,1024]{2,1,0:T(8,128)S(1)}, f32[4,192,1024]{2,1,0:T(8,128)}, u32[]{:S(2)}, u32[]{:S(2)}) collective-permute-start(f32[4,192,1024]{2,1,0:T(8,128)S(1)} %slice.11), channel_id=1, source_target_pairs={{0,4},{4,0},{1,5},{5,1},{2,6},{6,2},{3,7},{7,3},{8,12},{12,8},{9,1... | collective-permute-start | bytes 9437192 | tf_op jit(solution)/shard_map/ppermute | solution.py:179
  172.5 21.6 %all-to-all-start.3 = ((f32[16,8,128]{2,1,0:T(8,128)}), f32[16,8,128]{2,1,0:T(8,128)S(1)}, u32[]{:S(2)}, u32[]{:S(2)}) async-start(f32[16,8,128]{2,1,0:T(8,128)} %broadcast_in_dim.5), calls=%async_computation.3 | async-start | bytes 131072 | tf_op jit(solution)/shard_map/all_to_all | solution.py:147
  194.1 39.7 %all-to-all-start.5 = ((f32[4,192,1024]{2,1,0:T(8,128)}), f32[4,192,1024]{2,1,0:T(8,128)S(1)}, u32[]{:S(2)}, u32[]{:S(2)}) async-start(f32[4,192,1024]{2,1,0:T(8,128)} %slice_add_fusion), calls=%async_computation.5 | async-start | bytes 6291456 | tf_op jit(solution)/shard_map/all_to_all | solution.py:181
Sparse Core Ops, SparseCore 0:
  10.1 77.5 all-gather.1
  155.1 77.8 reduce-scatter.1

commit v2 on v0

v2 whole, which is shorter than its diff:
```python
import jax
import jax.numpy as jnp
from jax import lax
from jax.experimental import pallas as pl
from jax.experimental.pallas import tpu as pltpu
from jax.sharding import Mesh, PartitionSpec as P

NZ, NY, NC, NX = 16, 4, 2, 4
NB = NY * NC
QBLK = 192
PBLK = 16
PB_DEV = 4
GROUP = PBLK * PB_DEV
QUERIES = NZ * NB * QBLK
CAND = NZ * PBLK
SHARE = NB * QBLK // NX
SENT = SHARE + 16
PER_X = NB // NX
LANES = 128
DP = ("z", "y", "core")
COL = ("y", "core")


def in_hbm(array):
    return pltpu.with_memory_space_constraint(array, pltpu.HBM)


def pick_rows(sel_ref, p_ref, chosen, b):
    for z in range(NZ):
        start = pl.multiple_of(z * GROUP + sel_ref[z, b] * PBLK, PBLK)
        chosen[z * PBLK : (z + 1) * PBLK, :] = p_ref[pl.ds(start, PBLK), :]


def encode_kernel(p_ref, pick_ref, q_ref, pos_ref, code_ref, out_ref):
    width = p_ref.shape[1]
    rows = p_ref[...].astype(jnp.float32)
    largest = jnp.maximum(jnp.max(jnp.abs(rows), axis=1, keepdims=True), 2.0**-126)
    shift = 13.0 - jnp.floor(jnp.log2(largest))
    half = jnp.floor(shift * 0.5)
    code_ref[:, :width] = rows * jnp.exp2(half) * jnp.exp2(shift - half)
    lane = lax.broadcasted_iota(jnp.int32, (GROUP, LANES), 1)
    spare = jnp.where(lane == LANES - 1, shift, 0.0)
    code_ref[:, width:] = spare
    picks = jnp.broadcast_to(pick_ref[...].astype(jnp.float32), (8, LANES))
    row = lax.broadcasted_iota(jnp.int32, (8, LANES), 0)
    picks = jnp.where(row == 0, picks, pltpu.roll(picks, LANES // 2, 1))
    code_ref[:8, width:] = jnp.where(lane[:8] < LANES // 2, picks, spare[:8])
    out_ref[:, :width] = q_ref[...]
    row = lax.broadcasted_iota(jnp.int32, (QBLK, QBLK), 0)
    col = lax.broadcasted_iota(jnp.int32, (QBLK, QBLK), 1)
    pos = jnp.where(row == col, pos_ref[...].astype(jnp.float32), 0.0)
    pos = jnp.sum(pos, axis=1, keepdims=True)
    high = jnp.floor(pos * (1.0 / LANES))
    lane = lax.broadcasted_iota(jnp.int32, (QBLK, LANES), 1)
    digits = jnp.where(lane == 0, high, jnp.where(lane == 1, pos - high * LANES, 0.0))
    out_ref[:, width:] = digits.astype(jnp.bfloat16)


def encode(passages, pair_block, queries, positives):
    rows, width = passages.shape
    scaled, marked = pl.pallas_call(
        encode_kernel,
        out_shape=(
            jax.ShapeDtypeStruct((rows, width + LANES), jnp.float32),
            jax.ShapeDtypeStruct((QBLK, width + LANES), jnp.bfloat16),
        ),
        compiler_params=pltpu.CompilerParams(vmem_limit_bytes=8 << 20),
        cost_estimate=pl.CostEstimate(
            flops=4 * rows * width, bytes_accessed=6 * rows * width, transcendentals=3 * rows
        ),
        name="encode",
    )(
        in_hbm(passages),
        in_hbm(pair_block.reshape(1, NZ * NB)),
        in_hbm(queries),
        in_hbm(positives.reshape(1, QBLK)),
    )
    return scaled.astype(jnp.float16), marked

def scores_kernel(at_ref, q_ref, c_ref, s_ref, p_ref, sel_ref, coded, held, passages, scores, chosen, picks, picked, sems):
    width = p_ref.shape[1]
    chunk = NZ * GROUP // NB

    def fetch_code(b):
        at = pl.ds(b * chunk, chunk)
        return pltpu.make_async_copy(c_ref.at[at], coded.at[at], sems.at[3, b])

    def fetch(b):
        return pltpu.make_async_copy(q_ref.at[b, :, pl.ds(0, width)], held.at[b], sems.at[0, b])

    def keep(b):
        at = pl.ds(b * chunk, chunk)
        return pltpu.make_async_copy(passages.at[at], p_ref.at[at], sems.at[1, b])

    def send(b):
        at = pl.ds(b * QBLK, QBLK)
        return pltpu.make_async_copy(scores.at[at], s_ref.at[at], sems.at[2, b])

    for b in range(NB):
        fetch_code(b).start()
    for b in range(NB):
        fetch(b).start()
    first = lax.rem(at_ref[0], LANES // 2)
    lower = at_ref[0] < LANES // 2
    for b in range(NB):
        fetch_code(b).wait()
        for z in range(b * chunk // GROUP, (b + 1) * chunk // GROUP):
            spare = coded[z * GROUP : z * GROUP + PBLK, width:].astype(jnp.int32)
            picks[z : z + 1, :] = jnp.where(lower, spare[:1], spare[1:2])
        at = pl.ds(b * chunk, chunk)
        code = coded[at]
        shift = code[:, width:][:, LANES - 1 :].astype(jnp.float32)
        half = jnp.floor(shift * 0.5)
        low, high = jnp.exp2(half - shift), jnp.exp2(-half)
        passages[at] = (code[:, :width].astype(jnp.float32) * low * high).astype(jnp.bfloat16)
        keep(b).start()
    picks[...] = pltpu.roll(picks[...], LANES - first, 1)
    local = pltpu.make_async_copy(picks, picked, sems.at[4, 0])
    local.start()
    local.wait()
    tell = pltpu.make_async_copy(picks, sel_ref, sems.at[4, 1])
    tell.start()
    for b in range(NB):
        pick_rows(picked, passages, chosen, b)
        fetch(b).wait()
        scores[pl.ds(b * QBLK, QBLK), :] = lax.dot_general(
            held[b], chosen[...], (((1,), (1,)), ((), ())), preferred_element_type=jnp.float32
        )
        send(b).start()
    tell.wait()
    for b in range(NB):
        keep(b).wait()
        send(b).wait()


def partial_scores(at, q_all, coded):
    width = q_all.shape[2] - LANES
    apart = pl.BlockSpec(memory_space=pl.ANY)
    return pl.pallas_call(
        scores_kernel,
        out_shape=(
            pltpu.HBM((NB * QBLK, CAND), jnp.float32),
            pltpu.HBM((NZ * GROUP, width), jnp.bfloat16),
            pltpu.HBM((NZ, LANES), jnp.int32),
        ),
        in_specs=[pl.BlockSpec(memory_space=pltpu.SMEM), apart, apart],
        out_specs=(apart, apart, apart),
        scratch_shapes=[
            pltpu.VMEM((NZ * GROUP, width + LANES), jnp.bfloat16),
            pltpu.VMEM((NB, QBLK, width), jnp.bfloat16),
            pltpu.VMEM((NZ * GROUP, width), jnp.bfloat16),
            pltpu.VMEM((NB * QBLK, CAND), jnp.float32),
            pltpu.VMEM((CAND, width), jnp.bfloat16),
            pltpu.VMEM((NZ, LANES), jnp.int32),
            pltpu.SMEM((NZ, LANES), jnp.int32),
            pltpu.SemaphoreType.DMA((5, NB)),
        ],
        compiler_params=pltpu.CompilerParams(vmem_limit_bytes=20 << 20),
        cost_estimate=pl.CostEstimate(
            flops=2 * NB * QBLK * CAND * width,
            bytes_accessed=2 * (NB * QBLK + 2 * NZ * GROUP) * width + 4 * NB * QBLK * CAND,
            transcendentals=0,
        ),
        name="partial_scores",
    )(at, in_hbm(q_all), in_hbm(coded))


def hits_of(digit_ref, col):
    digits = digit_ref[...].astype(jnp.float32)
    pos = (digits[:, :1] * LANES + digits[:, 1:2]).astype(jnp.int32)
    lane = lax.broadcasted_iota(jnp.int32, (SHARE, CAND), 1)
    return ((lane // PBLK) * NB + col) * PBLK + lane % PBLK == pos


def stats_kernel(col_ref, part_ref, digit_ref, s_ref, hit_ref, stat_ref):
    scores = (part_ref[0] + part_ref[1]) + (part_ref[2] + part_ref[3])
    s_ref[...] = scores
    top = jnp.max(scores, axis=1, keepdims=True)
    total = jnp.sum(jnp.exp(scores - top), axis=1, keepdims=True)
    hits = hits_of(digit_ref, col_ref[0])
    hit_ref[...] = hits.astype(jnp.float32)
    chosen = jnp.sum(jnp.where(hits, scores, 0.0), axis=1, keepdims=True)
    lane = lax.broadcasted_iota(jnp.int32, (SHARE, LANES), 1)
    packed = jnp.where(lane == 0, top, jnp.where(lane == 1, total, jnp.where(lane == 2, chosen, 0.0)))
    rows = packed.T[:8]
    for j in range(NB):
        stat_ref[j] = rows


def column_stats(col, parts, digits):
    return pl.pallas_call(
        stats_kernel,
        out_shape=(
            jax.ShapeDtypeStruct((SHARE, CAND), jnp.float32),
            jax.ShapeDtypeStruct((SHARE, CAND), jnp.float32),
            jax.ShapeDtypeStruct((NB, 8, SHARE), jnp.float32),
        ),
        in_specs=[
            pl.BlockSpec(memory_space=pltpu.SMEM),
            pl.BlockSpec(memory_space=pltpu.VMEM),
            pl.BlockSpec(memory_space=pltpu.VMEM),
        ],
        compiler_params=pltpu.CompilerParams(vmem_limit_bytes=8 << 20),
        cost_estimate=pl.CostEstimate(
            flops=12 * SHARE * CAND, bytes_accessed=20 * SHARE * CAND, transcendentals=SHARE * CAND
        ),
        name="column_stats",
    )(col, parts, in_hbm(digits))


def weigh_kernel(s_ref, hit_ref, stat_ref, w_ref):
    tops, totals, picked = stat_ref[:, 0, :], stat_ref[:, 1, :], stat_ref[:, 2, :]
    top = jnp.max(tops, axis=0, keepdims=True)
    total = jnp.sum(totals * jnp.exp(tops - top), axis=0, keepdims=True)
    losses = top + jnp.log(total) - jnp.sum(picked, axis=0, keepdims=True)
    row = lax.broadcasted_iota(jnp.int32, (LANES, SHARE), 0)
    turned = jnp.where(row == 0, top, jnp.where(row == 1, total, 0.0)).T
    probs = jnp.exp(s_ref[...] - turned[:, :1]) / turned[:, 1:2]
    w_ref[:SHARE] = (probs - hit_ref[...]).astype(jnp.bfloat16)
    loss = jnp.sum(losses, axis=1, keepdims=True)
    first = loss.astype(jnp.bfloat16).astype(jnp.float32)
    second = (loss - first).astype(jnp.bfloat16).astype(jnp.float32)
    row = lax.broadcasted_iota(jnp.int32, (SENT - SHARE, CAND), 0)
    pieces = jnp.where(row == 1, second, jnp.where(row == 2, loss - first - second, 0.0))
    w_ref[SHARE:] = jnp.where(row == 0, first, pieces).astype(jnp.bfloat16)


def weigh(scores, hits, stats):
    return pl.pallas_call(
        weigh_kernel,
        out_shape=jax.ShapeDtypeStruct((SENT, CAND), jnp.bfloat16),
        compiler_params=pltpu.CompilerParams(vmem_limit_bytes=8 << 20),
        cost_estimate=pl.CostEstimate(
            flops=10 * SHARE * CAND, bytes_accessed=6 * SHARE * CAND, transcendentals=SHARE * CAND
        ),
        name="weigh",
    )(scores, hits, stats)


def block_weights(w_ref, b):
    start = pl.multiple_of(lax.rem(b, PER_X) * QBLK, QBLK)
    return w_ref[lax.div(b, PER_X), pl.ds(start, QBLK), :]


def passage_kernel(sel_ref, q_ref, w_ref, pg_ref, kept_ref, acc, sems):
    width = acc.shape[1]
    keep = pltpu.make_async_copy(w_ref, kept_ref, sems.at[NZ])
    keep.start()
    acc[...] = jnp.zeros_like(acc)

    def add(b, done):
        cand = lax.dot_general(
            block_weights(w_ref, b),
            q_ref[b][:, :width],
            (((0,), (0,)), ((), ())),
            preferred_element_type=jnp.float32,
        )
        for z in range(NZ):
            start = pl.multiple_of(z * GROUP + sel_ref[z, b] * PBLK, PBLK)
            acc[pl.ds(start, PBLK), :] += cand[z * PBLK : (z + 1) * PBLK, :]
            done(z)

    def send(z):
        at = pl.ds(z * GROUP, GROUP)
        return pltpu.make_async_copy(acc.at[at], pg_ref.at[at], sems.at[z])

    lax.fori_loop(0, NB - 1, lambda b, carry: add(b, lambda z: None), None)
    add(jnp.int32(NB - 1), lambda z: send(z).start())
    for z in range(NZ):
        send(z).wait()
    keep.wait()


def passage_part(sel, q_all, weights):
    width = q_all.shape[2] - LANES
    whole = pl.BlockSpec(memory_space=pltpu.VMEM)
    apart = pl.BlockSpec(memory_space=pl.ANY)
    return pl.pallas_call(
        passage_kernel,
        out_shape=(
            pltpu.HBM((NZ * GROUP, width), jnp.float32),
            pltpu.HBM(weights.shape, weights.dtype),
        ),
        grid_spec=pltpu.PrefetchScalarGridSpec(
            num_scalar_prefetch=1,
            grid=(),
            in_specs=[whole, whole],
            out_specs=(apart, apart),
            scratch_shapes=[
                pltpu.VMEM((NZ * GROUP, width), jnp.float32),
                pltpu.SemaphoreType.DMA((NZ + 1,)),
            ],
        ),
        compiler_params=pltpu.CompilerParams(vmem_limit_bytes=16 << 20),
        cost_estimate=pl.CostEstimate(
            flops=2 * NB * QBLK * CAND * width,
            bytes_accessed=(2 * NB * QBLK + 4 * NZ * GROUP) * width + 2 * NB * QBLK * CAND,
            transcendentals=0,
        ),
        name="passage_part",
    )(sel, q_all, weights)


def query_kernel(sel_ref, tab_ref, p_ref, w_ref, *rest):
    *arrived, qg_ref, chosen = rest
    b = tab_ref[pl.program_id(0)]
    pick_rows(sel_ref, p_ref, chosen, b)
    share = jnp.dot(block_weights(w_ref, b), chosen[...], preferred_element_type=jnp.float32)
    qg_ref[0] = share + arrived[0][0] if arrived else share


def query_part(sel, tab, p_all, weights, *arrived):
    width = p_all.shape[1]
    block = pl.BlockSpec((1, QBLK, width), lambda k, sel, tab: (k, 0, 0))
    return pl.pallas_call(
        query_kernel,
        out_shape=jax.ShapeDtypeStruct((NY, QBLK, width), jnp.float32),
        grid_spec=pltpu.PrefetchScalarGridSpec(
            num_scalar_prefetch=2,
            grid=(NY,),
            in_specs=[
                pl.BlockSpec((NZ * GROUP, width), lambda k, sel, tab: (0, 0)),
                pl.BlockSpec((NX, SENT, CAND), lambda k, sel, tab: (0, 0, 0)),
            ]
            + [block] * len(arrived),
            out_specs=block,
            scratch_shapes=[pltpu.VMEM((CAND, width), jnp.bfloat16)],
        ),
        compiler_params=pltpu.CompilerParams(vmem_limit_bytes=16 << 20),
        cost_estimate=pl.CostEstimate(
            flops=2 * NY * QBLK * CAND * width,
            bytes_accessed=(4 * NY * QBLK + 2 * NZ * GROUP) * width + 2 * NB * QBLK * CAND,
            transcendentals=0,
        ),
        name="query_part",
    )(sel, tab, in_hbm(p_all), in_hbm(weights), *arrived)


def total_over(value, axis, size):
    copies = jnp.broadcast_to(value[None], (size,) + value.shape)
    return jnp.sum(lax.all_to_all(copies, axis, split_axis=0, concat_axis=0, tiled=True), axis=0)


def per_device(queries, passages, pair_block, positives):
    z, core, x = lax.axis_index("z"), lax.axis_index("core"), lax.axis_index("x")
    width = queries.shape[1]
    col = (lax.axis_index("y") * NC + core).astype(jnp.int32).reshape(1)
    code, marked = encode(passages, pair_block, queries, positives)
    q_all = lax.all_gather(marked, COL, axis=0, tiled=False)
    coded = lax.all_gather(code, "z", axis=0, tiled=True).astype(jnp.bfloat16)
    part, p_all, sel = partial_scores((z * NB).astype(jnp.int32).reshape(1), q_all, coded)
    digits = lax.dynamic_slice(q_all, (x * PER_X, 0, width), (PER_X, QBLK, LANES)).reshape(SHARE, LANES)
    parts = lax.all_to_all(
        part.reshape(NX, SHARE, CAND), "x", split_axis=0, concat_axis=0, tiled=True
    )
    scores, hits, stats = column_stats(col, parts, digits)
    stats = lax.all_to_all(stats, COL, split_axis=0, concat_axis=0, tiled=True)
    weights = lax.all_gather(weigh(scores, hits, stats), "x", axis=0, tiled=False)
    loss = jnp.sum(weights[:, SHARE : SHARE + 3, :1].astype(jnp.float32))

    passages_part, weights = passage_part(sel, q_all, weights)
    passage_grad = lax.psum_scatter(passages_part, "z", scatter_dimension=0, tiled=True)
    mine = jnp.arange(NY, dtype=jnp.int32) * NC + core
    away = jnp.arange(NY, dtype=jnp.int32) * NC + (1 - core)
    arrived = lax.ppermute(query_part(sel, away, p_all, weights), "core", [(0, 1), (1, 0)])
    query_grad = jnp.sum(
        lax.all_to_all(
            query_part(sel, mine, p_all, weights, arrived),
            "y",
            split_axis=0,
            concat_axis=0,
            tiled=True,
        ),
        axis=0,
    )
    loss = total_over(jnp.full((8, LANES), loss), "z", NZ)[0, 0] / QUERIES
    return loss, query_grad, passage_grad


def solution(mesh):
    fine = Mesh(mesh.devices.reshape(NZ, NY, NC, NX), DP + ("x",))
    in_specs = (P(DP, "x"), P(DP, "x"), P(None, DP), P(DP))
    out_specs = (P(), P(DP, "x"), P(DP, "x"))
    return jax.shard_map(
        per_device, mesh=fine, in_specs=in_specs, out_specs=out_specs, check_vma=False
    )
```

time: 936 us -> 206 us (0.22)
  the two profiles are of different devices: /device:TPU:1 before, /device:TPU:4 now
where the time goes in v2:
time: 206 us
  blocking collectives  77 us (37%)
  waiting for transfers between devices  62 us (30%)
  Pallas kernels  27.6 us (13%)
  starting transfers between devices  16.4 us (8%)
  between operations  15.9 us (8%)
  other arithmetic  4.39 us (2%)
  local copies, waits for them, and re-layouts  2.45 us (1%)
    all_gather x1, blocking collectives, per_device(): coded = lax.all_gather(code, 'z', axis=0, tiled=True).astype(jnp.bfloat16)  52.2 us
    all_to_all x1, waiting for transfers between devices, per_device(): lax.all_to_all(query_part(sel, mine, p_all, weights, arrived), 'y', split...  35.3 us
    all_gather x1, blocking collectives, per_device(): lax.all_gather(weigh(scores, hits, stats), 'x', axis=0, tiled=False)  14.9 us
    all_to_all x1, waiting for transfers between devices, per_device(): lax.all_to_all(part.reshape(NX, SHARE, CAND), 'x', split_axis=0, concat_a...  12.7 us
    all_to_all x1, blocking collectives, per_device(): stats = lax.all_to_all(stats, COL, split_axis=0, concat_axis=0, tiled=True)  9.9 us
    pallas_call x2, Pallas kernels, query_part(): pl.pallas_call(query_kernel, out_shape=jax.ShapeDtypeStruct((NY, QBLK, wi...  9.85 us
    pallas_call x1, Pallas kernels, partial_scores(): pl.pallas_call(scores_kernel, out_shape=(pltpu.HBM((NB * QBLK, CAND), jnp...  7.49 us
    all_to_all x1, waiting for transfers between devices, total_over(): lax.all_to_all(copies, axis, split_axis=0, concat_axis=0, tiled=True)  7.3 us
  transfers between devices with their start and end apart: 6, of which 4 were waited for; matrix products, arithmetic and copies ran while one was open for 3% of the time, Pallas kernels for 5%

profile of v2, /device:TPU:4, one launch (start us, length us, event | category | flops | bytes accessed | tf_op | source)
XLA Modules:
  0.0 205.6 jit_solution(11988029555888861373)
XLA Ops:
  7.2 2.0 encode.1
  9.3 52.2 %all-gather.6 = f16[1024,1152]{1,0:T(8,128)(2,1)S(1)} all-gather(f16[64,1152]{1,0:T(8,128)(2,1)S(1)} %convert_element_type.9), channel_id=1, replica_groups=mesh['z'=16,'y'=4,'core'=2,'x'=4] {'z'}, dimensions={0}, use_global_device_ids=true | all-gather | bytes 2506752 | tf_op jit(solution)/shard_map/all_gather | solution.py:350
  61.4 1.8 convert_element_type.10.c_ref
  63.2 7.5 %partial_scores.1 = (f32[1536,256]{1,0:T(8,128)}, bf16[1024,1024]{1,0:T(8,128)(2,1)}, s32[16,128]{1,0:T(8,128)}) custom-call(s32[1]{0:T(128)} %bitcast.1.at_ref, bf16[8,192,1152]{2,1,0:T(8,128)(2,1)} %bitcast.9, bf16[1024,1152]{1,0:T(8,128)(2,1)} %convert_element_type.10.c_ref), custom_call_target="tpu_custom_call" | custom-call | flops 805306368 | bytes 8912896 | tf_op jit(solution)/shard_map/partial_scores/pallas_call | solution.py:139
  70.7 4.8 %all-to-all-start = ((f32[4,384,256]{2,1,0:T(8,128)}), f32[4,384,256]{2,1,0:T(8,128)}, u32[]{:S(2)}, u32[]{:S(2)}) async-start(f32[4,384,256]{2,1,0:T(8,128)} %bitcast.14), calls=%async_computation | async-start | bytes 3145728 | tf_op jit(solution)/shard_map/all_to_all | solution.py:353
  75.6 0.6 constant_dynamic-slice_fusion
  76.2 12.7 %all-to-all-done.part_ref = f32[4,384,256]{2,1,0:T(8,128)} async-done(((f32[4,384,256]{2,1,0:T(8,128)}), f32[4,384,256]{2,1,0:T(8,128)}, u32[]{:S(2)}, u32[]{:S(2)}) %all-to-all-start) | async-done | bytes 1572896 | tf_op jit(solution)/shard_map/all_to_all | solution.py:353
  88.9 1.9 column_stats.1
  90.9 9.9 %all_to_all.20.stat_ref = f32[8,8,384]{2,1,0:T(8,128)S(1)} all-to-all(f32[8,8,384]{2,1,0:T(8,128)S(1)} %get-tuple-element.18), channel_id=1, replica_groups=mesh['z'=16,'y'=4,'core'=2,'x'=4] {'y','core'}, dimensions={0} | all-to-all | bytes 196608 | tf_op jit(solution)/shard_map/all_to_all | solution.py:357
  100.8 0.4 weigh.1
  101.1 14.9 %all-gather.1 = bf16[1600,256]{1,0:T(8,128)(2,1)S(1)} all-gather(bf16[400,256]{1,0:T(8,128)(2,1)S(1)} %weigh.1), channel_id=3, replica_groups=mesh['z'=16,'y'=4,'core'=2,'x'=4] {'x'}, dimensions={0}, use_global_device_ids=true | all-gather | bytes 1024000 | tf_op jit(solution)/shard_map/all_gather | solution.py:358
  116.1 5.9 %passage_part.1 = (f32[1024,1024]{1,0:T(8,128)}, bf16[4,400,256]{2,1,0:T(8,128)(2,1)}) custom-call(s32[16,128]{1,0:T(8,128)S(1)} %copy-done.2, bf16[8,192,1152]{2,1,0:T(8,128)(2,1)S(1)} %bitcast.11, bf16[4,400,256]{2,1,0:T(8,128)(2,1)S(1)} %bitcast.12), custom_call_target="tpu_custom_call" | custom-call | flops 805306368 | bytes 8126464 | tf_op jit(solution)/shard_map/passage_part/pallas_call | solution.py:278
  122.0 3.6 %query_part.2 = f32[4,192,1024]{2,1,0:T(8,128)S(1)} custom-call(s32[16,128]{1,0:T(8,128)S(1)} %copy-done.2, s32[4]{0:T(128)S(1)} %fusion.tab_ref, bf16[1024,1024]{1,0:T(8,128)(2,1)} %get-tuple-element.20.p_ref, bf16[4,400,256]{2,1,0:T(8,128)(2,1)} %get-tuple-element.21.w_ref), custom_call_target="tpu_custom_call" | custom-call | flops 402653184 | bytes 6029312 | tf_op jit(solution)/shard_map/query_part/pallas_call | solution.py:315
  125.7 1.9 collective-permute-start
  127.6 1.3 convert_reduce_fusion
  128.9 1.3 broadcast_in_dim_broadcast_in_dim_broadcast_in_dim.3
  130.2 5.9 %all-to-all-start.2 = ((f32[16,8,128]{2,1,0:T(8,128)}), f32[16,8,128]{2,1,0:T(8,128)S(1)}, u32[]{:S(2)}, u32[]{:S(2)}) async-start(f32[16,8,128]{2,1,0:T(8,128)} %broadcast_in_dim_broadcast_in_dim_broadcast_in_dim.3), calls=%async_computation.2 | async-start | bytes 131072 | tf_op jit(solution)/shard_map/all_to_all | solution.py:341
  136.1 6.2 %query_part.3 = f32[4,192,1024]{2,1,0:T(8,128)} custom-call(s32[16,128]{1,0:T(8,128)S(1)} %copy-done.2, s32[4]{0:T(128)S(1)} %fusion.1.tab_ref, bf16[1024,1024]{1,0:T(8,128)(2,1)} %get-tuple-element.20.p_ref, bf16[4,400,256]{2,1,0:T(8,128)(2,1)} %get-tuple-element.21.w_ref, f32[4,192,1024]{2,1,0:T(8,128)} %collective-permute-done.rest_0_), custom_call_target="tpu_custom_call" | custom-call | flops 402653184 | bytes 6029312 | tf_op jit(solution)/shard_map/query_part/pallas_call | solution.py:315
  142.3 7.3 %all-to-all-done.2 = f32[16,8,128]{2,1,0:T(8,128)S(1)} async-done(((f32[16,8,128]{2,1,0:T(8,128)}), f32[16,8,128]{2,1,0:T(8,128)S(1)}, u32[]{:S(2)}, u32[]{:S(2)}) %all-to-all-start.2) | async-done | bytes 65568 | tf_op jit(solution)/shard_map/all_to_all | solution.py:341
  149.6 3.7 %all-to-all-start.3 = ((f32[4,192,1024]{2,1,0:T(8,128)}), f32[4,192,1024]{2,1,0:T(8,128)S(1)}, u32[]{:S(2)}, u32[]{:S(2)}) async-start(f32[4,192,1024]{2,1,0:T(8,128)} %query_part.3), calls=%async_computation.3 | async-start | bytes 6291456 | tf_op jit(solution)/shard_map/all_to_all | solution.py:367
  153.4 0.5 slice.7
  154.5 35.3 %all-to-all-done.3 = f32[4,192,1024]{2,1,0:T(8,128)S(1)} async-done(((f32[4,192,1024]{2,1,0:T(8,128)}), f32[4,192,1024]{2,1,0:T(8,128)S(1)}, u32[]{:S(2)}, u32[]{:S(2)}) %all-to-all-start.3) | async-done | bytes 3145760 | tf_op jit(solution)/shard_map/all_to_all | solution.py:367
  189.8 1.2 reduce_sum.29
  191.0 6.7 %reduce-scatter.2.cloned.1.call-done = f32[64,1024]{1,0:T(8,128)} async-done(((f32[1024,1024]{1,0:T(8,128)}), f32[64,1024]{1,0:T(8,128)}) %reduce-scatter.2.cloned.1.call-update) | async-done | bytes 262160 | tf_op jit(solution)/shard_map/reduce_scatter | solution.py:362
  (16 shorter events, 0.1 us)
Async XLA Ops:
  7.2 56.1 %all-gather.5.cloned.1.call-start = ((), (), s32[]{:S(2)}) async-start(), calls=%async_computation.6 | async-start | bytes 3981312 | tf_op jit(solution)/shard_map/all_gather | solution.py:349
  63.2 12.3 %copy-start = (bf16[1536,1152]{1,0:T(8,128)(2,1)S(1)}, bf16[1536,1152]{1,0:T(8,128)(2,1)}, u32[]{:S(2)}) copy-start(bf16[1536,1152]{1,0:T(8,128)(2,1)} %all-gather.5.cloned.1.call-done) | copy-start | bytes 10616836
  70.7 45.3 %copy-start.2 = (s32[16,128]{1,0:T(8,128)S(1)}, s32[16,128]{1,0:T(8,128)}, u32[]{:S(2)}) copy-start(s32[16,128]{1,0:T(8,128)} %get-tuple-element.19.sel_ref) | copy-start | bytes 24580
  70.7 18.2 %all-to-all-start = ((f32[4,384,256]{2,1,0:T(8,128)}), f32[4,384,256]{2,1,0:T(8,128)}, u32[]{:S(2)}, u32[]{:S(2)}) async-start(f32[4,384,256]{2,1,0:T(8,128)} %bitcast.14), calls=%async_computation | async-start | bytes 3145728 | tf_op jit(solution)/shard_map/all_to_all | solution.py:353
  75.6 122.1 %reduce-scatter.2.cloned.1.call-start = ((), (), s32[]{:S(2)}) async-start(), calls=%async_computation.5 | async-start | bytes 4456448 | tf_op jit(solution)/shard_map/reduce_scatter | solution.py:362
  116.1 5.9 %copy-start.1 = (bf16[1600,256]{1,0:T(8,128)(2,1)}, bf16[1600,256]{1,0:T(8,128)(2,1)S(1)}, u32[]{:S(2)}) copy-start(bf16[1600,256]{1,0:T(8,128)(2,1)S(1)} %all-gather.1) | copy-start | bytes 2457604
  125.7 10.4 %collective-permute-start = (f32[4,192,1024]{2,1,0:T(8,128)S(1)}, f32[4,192,1024]{2,1,0:T(8,128)}, u32[]{:S(2)}, u32[]{:S(2)}) collective-permute-start(f32[4,192,1024]{2,1,0:T(8,128)S(1)} %query_part.2), channel_id=1, source_target_pairs={{0,4},{4,0},{1,5},{5,1},{2,6},{6,2},{3,7},{7,3},{8,12},{12,8},{9,1... | collective-permute-start | bytes 9437192 | tf_op jit(solution)/shard_map/ppermute | solution.py:365
  130.2 19.4 %all-to-all-start.2 = ((f32[16,8,128]{2,1,0:T(8,128)}), f32[16,8,128]{2,1,0:T(8,128)S(1)}, u32[]{:S(2)}, u32[]{:S(2)}) async-start(f32[16,8,128]{2,1,0:T(8,128)} %broadcast_in_dim_broadcast_in_dim_broadcast_in_dim.3), calls=%async_computation.2 | async-start | bytes 131072 | tf_op jit(solution)/shard_map/all_to_all | solution.py:341
  149.6 40.2 %all-to-all-start.3 = ((f32[4,192,1024]{2,1,0:T(8,128)}), f32[4,192,1024]{2,1,0:T(8,128)S(1)}, u32[]{:S(2)}, u32[]{:S(2)}) async-start(f32[4,192,1024]{2,1,0:T(8,128)} %query_part.3), calls=%async_computation.3 | async-start | bytes 6291456 | tf_op jit(solution)/shard_map/all_to_all | solution.py:367
Sparse Core Ops, SparseCore 0:
  10.7 41.5 all-gather.4
  122.2 75.4 reduce-scatter.1

commit v3 on v2

--- a/solution.py
+++ b/solution.py
@@ -77,13 +77,13 @@
     )
     return scaled.astype(jnp.float16), marked
 
-def scores_kernel(at_ref, q_ref, c_ref, s_ref, p_ref, sel_ref, coded, held, passages, scores, chosen, picks, picked, sems):
+def scores_kernel(at_ref, q_ref, c_ref, s_ref, p_ref, sel_ref, coded, held, passages, chosen, spares, picks, picked, sems):
     width = p_ref.shape[1]
     chunk = NZ * GROUP // NB
 
     def fetch_code(b):
         at = pl.ds(b * chunk, chunk)
-        return pltpu.make_async_copy(c_ref.at[at], coded.at[at], sems.at[3, b])
+        return pltpu.make_async_copy(c_ref.at[at], coded.at[at], sems.at[2, b])
 
     def fetch(b):
         return pltpu.make_async_copy(q_ref.at[b, :, pl.ds(0, width)], held.at[b], sems.at[0, b])
@@ -92,21 +92,25 @@
         at = pl.ds(b * chunk, chunk)
         return pltpu.make_async_copy(passages.at[at], p_ref.at[at], sems.at[1, b])
 
-    def send(b):
-        at = pl.ds(b * QBLK, QBLK)
-        return pltpu.make_async_copy(scores.at[at], s_ref.at[at], sems.at[2, b])
-
+    side = pltpu.make_async_copy(c_ref.at[:, pl.ds(width, LANES)], spares, sems.at[3, 2])
+    side.start()
     for b in range(NB):
         fetch_code(b).start()
     for b in range(NB):
         fetch(b).start()
-    first = lax.rem(at_ref[0], LANES // 2)
-    lower = at_ref[0] < LANES // 2
+    first = lax.rem(at_ref[2], LANES // 2)
+    lower = at_ref[2] < LANES // 2
+    side.wait()
+    for z in range(NZ):
+        spare = spares[z * GROUP : z * GROUP + PBLK, :].astype(jnp.int32)
+        picks[z : z + 1, :] = jnp.where(lower, spare[:1], spare[1:2])
+    picks[...] = pltpu.roll(picks[...], LANES - first, 1)
+    local = pltpu.make_async_copy(picks, picked, sems.at[3, 0])
+    local.start()
+    tell = pltpu.make_async_copy(picks, sel_ref, sems.at[3, 1])
+    tell.start()
     for b in range(NB):
         fetch_code(b).wait()
-        for z in range(b * chunk // GROUP, (b + 1) * chunk // GROUP):
-            spare = coded[z * GROUP : z * GROUP + PBLK, width:].astype(jnp.int32)
-            picks[z : z + 1, :] = jnp.where(lower, spare[:1], spare[1:2])
         at = pl.ds(b * chunk, chunk)
         code = coded[at]
         shift = code[:, width:][:, LANES - 1 :].astype(jnp.float32)
@@ -114,23 +118,21 @@
         low, high = jnp.exp2(half - shift), jnp.exp2(-half)
         passages[at] = (code[:, :width].astype(jnp.float32) * low * high).astype(jnp.bfloat16)
         keep(b).start()
-    picks[...] = pltpu.roll(picks[...], LANES - first, 1)
-    local = pltpu.make_async_copy(picks, picked, sems.at[4, 0])
-    local.start()
     local.wait()
-    tell = pltpu.make_async_copy(picks, sel_ref, sems.at[4, 1])
-    tell.start()
-    for b in range(NB):
+
+    def step(b, carry):
         pick_rows(picked, passages, chosen, b)
         fetch(b).wait()
-        scores[pl.ds(b * QBLK, QBLK), :] = lax.dot_general(
+        at = pl.ds(pl.multiple_of(b * QBLK, QBLK), QBLK)
+        s_ref[at, :] = lax.dot_general(
             held[b], chosen[...], (((1,), (1,)), ((), ())), preferred_element_type=jnp.float32
         )
-        send(b).start()
+        return carry
+
+    lax.fori_loop(0, NB, step, None)
     tell.wait()
     for b in range(NB):
         keep(b).wait()
-        send(b).wait()
 
 
 def partial_scores(at, q_all, coded):
@@ -139,21 +141,21 @@
     return pl.pallas_call(
         scores_kernel,
         out_shape=(
-            pltpu.HBM((NB * QBLK, CAND), jnp.float32),
+            jax.ShapeDtypeStruct((NB * QBLK, CAND), jnp.float32),
             pltpu.HBM((NZ * GROUP, width), jnp.bfloat16),
             pltpu.HBM((NZ, LANES), jnp.int32),
         ),
         in_specs=[pl.BlockSpec(memory_space=pltpu.SMEM), apart, apart],
-        out_specs=(apart, apart, apart),
+        out_specs=(pl.BlockSpec(memory_space=pltpu.VMEM), apart, apart),
         scratch_shapes=[
             pltpu.VMEM((NZ * GROUP, width + LANES), jnp.bfloat16),
             pltpu.VMEM((NB, QBLK, width), jnp.bfloat16),
             pltpu.VMEM((NZ * GROUP, width), jnp.bfloat16),
-            pltpu.VMEM((NB * QBLK, CAND), jnp.float32),
             pltpu.VMEM((CAND, width), jnp.bfloat16),
+            pltpu.VMEM((NZ * GROUP, LANES), jnp.bfloat16),
             pltpu.VMEM((NZ, LANES), jnp.int32),
             pltpu.SMEM((NZ, LANES), jnp.int32),
-            pltpu.SemaphoreType.DMA((5, NB)),
+            pltpu.SemaphoreType.DMA((4, NB)),
         ],
         compiler_params=pltpu.CompilerParams(vmem_limit_bytes=20 << 20),
         cost_estimate=pl.CostEstimate(
@@ -165,19 +167,24 @@
     )(at, in_hbm(q_all), in_hbm(coded))
 
 
-def hits_of(digit_ref, col):
-    digits = digit_ref[...].astype(jnp.float32)
+def hits_of(digits, col):
+    digits = digits.astype(jnp.float32)
     pos = (digits[:, :1] * LANES + digits[:, 1:2]).astype(jnp.int32)
     lane = lax.broadcasted_iota(jnp.int32, (SHARE, CAND), 1)
     return ((lane // PBLK) * NB + col) * PBLK + lane % PBLK == pos
 
 
-def stats_kernel(col_ref, part_ref, digit_ref, s_ref, hit_ref, stat_ref):
+def stats_kernel(at_ref, part_ref, q_ref, s_ref, hit_ref, stat_ref, digits, sem):
+    width = q_ref.shape[2] - LANES
+    mine = q_ref.at[pl.ds(at_ref[1] * PER_X, PER_X), :, pl.ds(width, LANES)]
+    copy = pltpu.make_async_copy(mine, digits, sem)
+    copy.start()
     scores = (part_ref[0] + part_ref[1]) + (part_ref[2] + part_ref[3])
     s_ref[...] = scores
     top = jnp.max(scores, axis=1, keepdims=True)
     total = jnp.sum(jnp.exp(scores - top), axis=1, keepdims=True)
-    hits = hits_of(digit_ref, col_ref[0])
+    copy.wait()
+    hits = hits_of(digits[...].reshape(SHARE, LANES), at_ref[0])
     hit_ref[...] = hits.astype(jnp.float32)
     chosen = jnp.sum(jnp.where(hits, scores, 0.0), axis=1, keepdims=True)
     lane = lax.broadcasted_iota(jnp.int32, (SHARE, LANES), 1)
@@ -187,7 +194,7 @@
         stat_ref[j] = rows
 
 
-def column_stats(col, parts, digits):
+def column_stats(at, parts, q_all):
     return pl.pallas_call(
         stats_kernel,
         out_shape=(
@@ -198,14 +205,18 @@
         in_specs=[
             pl.BlockSpec(memory_space=pltpu.SMEM),
             pl.BlockSpec(memory_space=pltpu.VMEM),
-            pl.BlockSpec(memory_space=pltpu.VMEM),
+            pl.BlockSpec(memory_space=pl.ANY),
+        ],
+        scratch_shapes=[
+            pltpu.VMEM((PER_X, QBLK, LANES), jnp.bfloat16),
+            pltpu.SemaphoreType.DMA,
         ],
         compiler_params=pltpu.CompilerParams(vmem_limit_bytes=8 << 20),
         cost_estimate=pl.CostEstimate(
             flops=12 * SHARE * CAND, bytes_accessed=20 * SHARE * CAND, transcendentals=SHARE * CAND
         ),
         name="column_stats",
-    )(col, parts, in_hbm(digits))
+    )(at, parts, in_hbm(q_all))
 
 
 def weigh_kernel(s_ref, hit_ref, stat_ref, w_ref):
@@ -248,24 +259,28 @@
     keep.start()
     acc[...] = jnp.zeros_like(acc)
 
-    def add(b, done):
+    def add(b, part, done):
+        rows = CAND // 2
         cand = lax.dot_general(
-            block_weights(w_ref, b),
+            block_weights(w_ref, b)[:, part * rows : (part + 1) * rows],
             q_ref[b][:, :width],
             (((0,), (0,)), ((), ())),
             preferred_element_type=jnp.float32,
         )
-        for z in range(NZ):
+        for k in range(NZ // 2):
+            z = part * (NZ // 2) + k
             start = pl.multiple_of(z * GROUP + sel_ref[z, b] * PBLK, PBLK)
-            acc[pl.ds(start, PBLK), :] += cand[z * PBLK : (z + 1) * PBLK, :]
+            acc[pl.ds(start, PBLK), :] += cand[k * PBLK : (k + 1) * PBLK, :]
             done(z)
 
     def send(z):
         at = pl.ds(z * GROUP, GROUP)
         return pltpu.make_async_copy(acc.at[at], pg_ref.at[at], sems.at[z])
 
-    lax.fori_loop(0, NB - 1, lambda b, carry: add(b, lambda z: None), None)
-    add(jnp.int32(NB - 1), lambda z: send(z).start())
+    for part in range(2):
+        for b in range(NB - 1):
+            add(jnp.int32(b), part, lambda z: None)
+        add(jnp.int32(NB - 1), part, lambda z: send(z).start())
     for z in range(NZ):
         send(z).wait()
     keep.wait()
@@ -344,16 +359,15 @@
 def per_device(queries, passages, pair_block, positives):
     z, core, x = lax.axis_index("z"), lax.axis_index("core"), lax.axis_index("x")
     width = queries.shape[1]
-    col = (lax.axis_index("y") * NC + core).astype(jnp.int32).reshape(1)
+    at = jnp.stack([lax.axis_index("y") * NC + core, x, z * NB]).astype(jnp.int32)
     code, marked = encode(passages, pair_block, queries, positives)
     q_all = lax.all_gather(marked, COL, axis=0, tiled=False)
     coded = lax.all_gather(code, "z", axis=0, tiled=True).astype(jnp.bfloat16)
-    part, p_all, sel = partial_scores((z * NB).astype(jnp.int32).reshape(1), q_all, coded)
-    digits = lax.dynamic_slice(q_all, (x * PER_X, 0, width), (PER_X, QBLK, LANES)).reshape(SHARE, LANES)
+    part, p_all, sel = partial_scores(at, q_all, coded)
     parts = lax.all_to_all(
         part.reshape(NX, SHARE, CAND), "x", split_axis=0, concat_axis=0, tiled=True
     )
-    scores, hits, stats = column_stats(col, parts, digits)
+    scores, hits, stats = column_stats(at, parts, q_all)
     stats = lax.all_to_all(stats, COL, split_axis=0, concat_axis=0, tiled=True)
     weights = lax.all_gather(weigh(scores, hits, stats), "x", axis=0, tiled=False)
     loss = jnp.sum(weights[:, SHARE : SHARE + 3, :1].astype(jnp.float32))

time: 206 us -> 203 us (0.985)
  blocking collectives: 77 us -> 93.7 us
  waiting for transfers between devices: 62 us -> 48.7 us
  starting transfers between devices: 16.4 us -> 12.6 us
    all_to_all x0 -> x1, blocking collectives: none -> 17.8 us  [per_device(): lax.all_to_all(part.reshape(NX, SHARE, CAND), 'x', split_axis=0, concat_a...]
    all_to_all x1 -> x0, waiting for transfers between devices: 12.7 us -> none  [per_device(): lax.all_to_all(part.reshape(NX, SHARE, CAND), 'x', split_axis=0, concat_a...]
    all_to_all x1 -> x0, starting transfers between devices: 4.81 us -> none  [per_device(): lax.all_to_all(part.reshape(NX, SHARE, CAND), 'x', split_axis=0, concat_a...]
  transfers between devices with their start and end apart: 6 -> 5, of which waited for: 4 -> 3; matrix products, arithmetic and copies ran while one was open for 3% -> 3% of each run, Pallas kernels for 5% -> 6%
where the time goes in v3:
time: 203 us; the launch traced here: 202 us
  blocking collectives  93.7 us (46%)
  waiting for transfers between devices  48.7 us (24%)
  Pallas kernels  25.8 us (13%)
  between operations  15.9 us (8%)
  starting transfers between devices  12.6 us (6%)
  other arithmetic  3.73 us (2%)
    all_gather x1, blocking collectives, per_device(): coded = lax.all_gather(code, 'z', axis=0, tiled=True).astype(jnp.bfloat16)  52.2 us
    all_to_all x1, waiting for transfers between devices, per_device(): lax.all_to_all(query_part(sel, mine, p_all, weights, arrived), 'y', split...  35.2 us
    all_to_all x1, blocking collectives, per_device(): lax.all_to_all(part.reshape(NX, SHARE, CAND), 'x', split_axis=0, concat_a...  17.8 us
    all_gather x1, blocking collectives, per_device(): lax.all_gather(weigh(scores, hits, stats), 'x', axis=0, tiled=False)  14.7 us
    pallas_call x2, Pallas kernels, query_part(): pl.pallas_call(query_kernel, out_shape=jax.ShapeDtypeStruct((NY, QBLK, wi...  11.4 us
    all_to_all x1, blocking collectives, per_device(): stats = lax.all_to_all(stats, COL, split_axis=0, concat_axis=0, tiled=True)  9.03 us
    all_to_all x1, waiting for transfers between devices, total_over(): lax.all_to_all(copies, axis, split_axis=0, concat_axis=0, tiled=True)  7.26 us
    all_to_all x1, starting transfers between devices, total_over(): lax.all_to_all(copies, axis, split_axis=0, concat_axis=0, tiled=True)  6.87 us
  transfers between devices with their start and end apart: 5, of which 3 were waited for; matrix products, arithmetic and copies ran while one was open for 3% of the time, Pallas kernels for 6%

profile of v3, /device:TPU:4, one launch (start us, length us, event | category | flops | bytes accessed | tf_op | source)
XLA Modules:
  0.0 202.3 jit_solution(15204502301265427640)
XLA Ops:
  7.2 2.0 encode.1
  9.2 0.0 reduce-scatter.2.cloned.1.call-start
  9.3 52.2 %all-gather.6 = f16[1024,1152]{1,0:T(8,128)(2,1)S(1)} all-gather(f16[64,1152]{1,0:T(8,128)(2,1)S(1)} %convert_element_type.9), channel_id=1, replica_groups=mesh['z'=16,'y'=4,'core'=2,'x'=4] {'z'}, dimensions={0}, use_global_device_ids=true | all-gather | bytes 2506752 | tf_op jit(solution)/shard_map/all_gather | solution.py:365
  61.5 1.8 convert_element_type.10.c_ref
  63.3 0.1 pad_add_fusion.at_ref
  63.3 5.9 %partial_scores.1 = (f32[1536,256]{1,0:T(8,128)S(1)}, bf16[1024,1024]{1,0:T(8,128)(2,1)}, s32[16,128]{1,0:T(8,128)}) custom-call(s32[3]{0:T(128)S(1)} %pad_add_fusion.at_ref, bf16[8,192,1152]{2,1,0:T(8,128)(2,1)} %bitcast.9, bf16[1024,1152]{1,0:T(8,128)(2,1)} %convert_element_type.10.c_ref), custom_call_target="tpu_custom_call" | custom-call | flops 805306368 | bytes 8912896 | tf_op jit(solution)/shard_map/partial_scores/pallas_call | solution.py:141
  69.2 17.8 %all_to_all.20.part_ref = f32[4,384,256]{2,1,0:T(8,128)S(1)} all-to-all(f32[4,384,256]{2,1,0:T(8,128)S(1)} %bitcast.14), channel_id=1, replica_groups=mesh['z'=16,'y'=4,'core'=2,'x'=4] {'x'}, dimensions={0} | all-to-all | bytes 3145728 | tf_op jit(solution)/shard_map/all_to_all | solution.py:367
  87.1 2.3 %column_stats.1 = (f32[384,256]{1,0:T(8,128)S(1)}, f32[384,256]{1,0:T(8,128)S(1)}, f32[8,8,384]{2,1,0:T(8,128)S(1)}) custom-call(s32[3]{0:T(128)S(1)} %pad_add_fusion.at_ref, f32[4,384,256]{2,1,0:T(8,128)S(1)} %all_to_all.20.part_ref, bf16[8,192,1152]{2,1,0:T(8,128)(2,1)} %bitcast.10), custom_call_target="tpu_custom_call" | custom-call | flops 1179648 | bytes 1966080 | tf_op jit(solution)/shard_map/column_stats/pallas_call | solution.py:198
  89.3 9.0 %all_to_all.21.stat_ref = f32[8,8,384]{2,1,0:T(8,128)S(1)} all-to-all(f32[8,8,384]{2,1,0:T(8,128)S(1)} %get-tuple-element.18), channel_id=1, replica_groups=mesh['z'=16,'y'=4,'core'=2,'x'=4] {'y','core'}, dimensions={0} | all-to-all | bytes 196608 | tf_op jit(solution)/shard_map/all_to_all | solution.py:371
  98.4 0.4 weigh.1
  98.7 14.7 %all-gather.1 = bf16[1600,256]{1,0:T(8,128)(2,1)S(1)} all-gather(bf16[400,256]{1,0:T(8,128)(2,1)S(1)} %weigh.1), channel_id=3, replica_groups=mesh['z'=16,'y'=4,'core'=2,'x'=4] {'x'}, dimensions={0}, use_global_device_ids=true | all-gather | bytes 1024000 | tf_op jit(solution)/shard_map/all_gather | solution.py:372
  113.4 3.9 %passage_part.1 = (f32[1024,1024]{1,0:T(8,128)}, bf16[4,400,256]{2,1,0:T(8,128)(2,1)}) custom-call(s32[16,128]{1,0:T(8,128)S(1)} %copy-done.1, bf16[8,192,1152]{2,1,0:T(8,128)(2,1)S(1)} %bitcast.11, bf16[4,400,256]{2,1,0:T(8,128)(2,1)S(1)} %bitcast.12), custom_call_target="tpu_custom_call" | custom-call | flops 805306368 | bytes 8126464 | tf_op jit(solution)/shard_map/passage_part/pallas_call | solution.py:293
  117.4 5.2 %query_part.2 = f32[4,192,1024]{2,1,0:T(8,128)} custom-call(s32[16,128]{1,0:T(8,128)S(1)} %copy-done.1, s32[4]{0:T(128)S(1)} %fusion.tab_ref, bf16[1024,1024]{1,0:T(8,128)(2,1)} %get-tuple-element.20.p_ref, bf16[4,400,256]{2,1,0:T(8,128)(2,1)} %get-tuple-element.21.w_ref), custom_call_target="tpu_custom_call" | custom-call | flops 402653184 | bytes 6029312 | tf_op jit(solution)/shard_map/query_part/pallas_call | solution.py:330
  122.6 1.9 collective-permute-start
  124.5 0.6 convert_reduce_fusion
  125.1 1.3 broadcast_in_dim_broadcast_in_dim_broadcast_in_dim.3
  126.4 6.9 %all-to-all-start.2 = ((f32[16,8,128]{2,1,0:T(8,128)}), f32[16,8,128]{2,1,0:T(8,128)S(1)}, u32[]{:S(2)}, u32[]{:S(2)}) async-start(f32[16,8,128]{2,1,0:T(8,128)} %broadcast_in_dim_broadcast_in_dim_broadcast_in_dim.3), calls=%async_computation.2 | async-start | bytes 131072 | tf_op jit(solution)/shard_map/all_to_all | solution.py:356
  133.2 6.3 %query_part.3 = f32[4,192,1024]{2,1,0:T(8,128)} custom-call(s32[16,128]{1,0:T(8,128)S(1)} %copy-done.1, s32[4]{0:T(128)S(1)} %fusion.1.tab_ref, bf16[1024,1024]{1,0:T(8,128)(2,1)} %get-tuple-element.20.p_ref, bf16[4,400,256]{2,1,0:T(8,128)(2,1)} %get-tuple-element.21.w_ref, f32[4,192,1024]{2,1,0:T(8,128)} %collective-permute-done.rest_0_), custom_call_target="tpu_custom_call" | custom-call | flops 402653184 | bytes 6029312 | tf_op jit(solution)/shard_map/query_part/pallas_call | solution.py:330
  139.5 7.3 %all-to-all-done.2 = f32[16,8,128]{2,1,0:T(8,128)S(1)} async-done(((f32[16,8,128]{2,1,0:T(8,128)}), f32[16,8,128]{2,1,0:T(8,128)S(1)}, u32[]{:S(2)}, u32[]{:S(2)}) %all-to-all-start.2) | async-done | bytes 65568 | tf_op jit(solution)/shard_map/all_to_all | solution.py:356
  146.8 3.7 %all-to-all-start.3 = ((f32[4,192,1024]{2,1,0:T(8,128)}), f32[4,192,1024]{2,1,0:T(8,128)S(1)}, u32[]{:S(2)}, u32[]{:S(2)}) async-start(f32[4,192,1024]{2,1,0:T(8,128)} %query_part.3), calls=%async_computation.3 | async-start | bytes 6291456 | tf_op jit(solution)/shard_map/all_to_all | solution.py:381
  150.5 0.5 slice.7
  151.7 35.2 %all-to-all-done.3 = f32[4,192,1024]{2,1,0:T(8,128)S(1)} async-done(((f32[4,192,1024]{2,1,0:T(8,128)}), f32[4,192,1024]{2,1,0:T(8,128)S(1)}, u32[]{:S(2)}, u32[]{:S(2)}) %all-to-all-start.3) | async-done | bytes 3145760 | tf_op jit(solution)/shard_map/all_to_all | solution.py:381
  186.8 1.2 reduce_sum.29
  188.0 6.3 %reduce-scatter.2.cloned.1.call-done = f32[64,1024]{1,0:T(8,128)} async-done(((f32[1024,1024]{1,0:T(8,128)}), f32[64,1024]{1,0:T(8,128)}) %reduce-scatter.2.cloned.1.call-update) | async-done | bytes 262160 | tf_op jit(solution)/shard_map/reduce_scatter | solution.py:376
  (13 shorter events, 0.1 us)
Async XLA Ops:
  7.2 56.2 %all-gather.5.cloned.1.call-start = ((), (), s32[]{:S(2)}) async-start(), calls=%async_computation.6 | async-start | bytes 3981312 | tf_op jit(solution)/shard_map/all_gather | solution.py:364
  9.2 185.1 %reduce-scatter.2.cloned.1.call-start = ((), (), s32[]{:S(2)}) async-start(), calls=%async_computation.5 | async-start | bytes 4456448 | tf_op jit(solution)/shard_map/reduce_scatter | solution.py:376
  87.1 26.4 %copy-start = (bf16[1536,1152]{1,0:T(8,128)(2,1)S(1)}, bf16[1536,1152]{1,0:T(8,128)(2,1)}, u32[]{:S(2)}) copy-start(bf16[1536,1152]{1,0:T(8,128)(2,1)} %all-gather.5.cloned.1.call-done) | copy-start | bytes 10616836
  87.1 26.4 %copy-start.1 = (s32[16,128]{1,0:T(8,128)S(1)}, s32[16,128]{1,0:T(8,128)}, u32[]{:S(2)}) copy-start(s32[16,128]{1,0:T(8,128)} %get-tuple-element.19.sel_ref) | copy-start | bytes 24580
  122.6 10.7 %collective-permute-start = (f32[4,192,1024]{2,1,0:T(8,128)}, f32[4,192,1024]{2,1,0:T(8,128)}, u32[]{:S(2)}, u32[]{:S(2)}) collective-permute-start(f32[4,192,1024]{2,1,0:T(8,128)} %query_part.2), channel_id=1, source_target_pairs={{0,4},{4,0},{1,5},{5,1},{2,6},{6,2},{3,7},{7,3},{8,12},{12,8},{9,1... | collective-permute-start | bytes 9437192 | tf_op jit(solution)/shard_map/ppermute | solution.py:379
  126.4 20.4 %all-to-all-start.2 = ((f32[16,8,128]{2,1,0:T(8,128)}), f32[16,8,128]{2,1,0:T(8,128)S(1)}, u32[]{:S(2)}, u32[]{:S(2)}) async-start(f32[16,8,128]{2,1,0:T(8,128)} %broadcast_in_dim_broadcast_in_dim_broadcast_in_dim.3), calls=%async_computation.2 | async-start | bytes 131072 | tf_op jit(solution)/shard_map/all_to_all | solution.py:356
  146.8 40.1 %all-to-all-start.3 = ((f32[4,192,1024]{2,1,0:T(8,128)}), f32[4,192,1024]{2,1,0:T(8,128)S(1)}, u32[]{:S(2)}, u32[]{:S(2)}) async-start(f32[4,192,1024]{2,1,0:T(8,128)} %query_part.3), calls=%async_computation.3 | async-start | bytes 6291456 | tf_op jit(solution)/shard_map/all_to_all | solution.py:381
Sparse Core Ops, SparseCore 0:
  10.7 41.5 all-gather.4
  117.5 76.7 reduce-scatter.1

commit v4 on v3

--- a/solution.py
+++ b/solution.py
@@ -16,6 +16,8 @@
 SHARE = NB * QBLK // NX
 SENT = SHARE + 16
 PER_X = NB // NX
+HALVES = 2
+TILES = GROUP // PBLK
 LANES = 128
 DP = ("z", "y", "core")
 COL = ("y", "core")
@@ -37,14 +39,19 @@
     largest = jnp.maximum(jnp.max(jnp.abs(rows), axis=1, keepdims=True), 2.0**-126)
     shift = 13.0 - jnp.floor(jnp.log2(largest))
     half = jnp.floor(shift * 0.5)
-    code_ref[:, :width] = rows * jnp.exp2(half) * jnp.exp2(shift - half)
-    lane = lax.broadcasted_iota(jnp.int32, (GROUP, LANES), 1)
-    spare = jnp.where(lane == LANES - 1, shift, 0.0)
-    code_ref[:, width:] = spare
-    picks = jnp.broadcast_to(pick_ref[...].astype(jnp.float32), (8, LANES))
-    row = lax.broadcasted_iota(jnp.int32, (8, LANES), 0)
-    picks = jnp.where(row == 0, picks, pltpu.roll(picks, LANES // 2, 1))
-    code_ref[:8, width:] = jnp.where(lane[:8] < LANES // 2, picks, spare[:8])
+    scaled = rows * jnp.exp2(half) * jnp.exp2(shift - half)
+    slabs = width // LANES * TILES
+    for s in range(slabs):
+        t, j = s // TILES, s % TILES
+        code_ref[s] = scaled[j * PBLK : (j + 1) * PBLK, t * LANES : (t + 1) * LANES]
+    picks = jnp.broadcast_to(pick_ref[...].astype(jnp.float32), (PBLK, LANES))
+    row = lax.broadcasted_iota(jnp.int32, (PBLK, LANES), 0)
+    lane = lax.broadcasted_iota(jnp.int32, (PBLK, LANES), 1)
+    spare = jnp.where(row == 0, picks, pltpu.roll(picks, LANES // 2, 1))
+    spare = jnp.where((row < 2) & (lane < LANES // 2), spare, 0.0)
+    for j in range(TILES):
+        spare = jnp.where(lane == LANES - TILES + j, shift[j * PBLK : (j + 1) * PBLK], spare)
+    code_ref[slabs] = spare
     out_ref[:, :width] = q_ref[...]
     row = lax.broadcasted_iota(jnp.int32, (QBLK, QBLK), 0)
     col = lax.broadcasted_iota(jnp.int32, (QBLK, QBLK), 1)
@@ -61,7 +68,7 @@
     scaled, marked = pl.pallas_call(
         encode_kernel,
         out_shape=(
-            jax.ShapeDtypeStruct((rows, width + LANES), jnp.float32),
+            jax.ShapeDtypeStruct((width // LANES * TILES + 1, PBLK, LANES), jnp.float32),
             jax.ShapeDtypeStruct((QBLK, width + LANES), jnp.bfloat16),
         ),
         compiler_params=pltpu.CompilerParams(vmem_limit_bytes=8 << 20),
@@ -81,8 +88,10 @@
     width = p_ref.shape[1]
     chunk = NZ * GROUP // NB
 
+    slabs = width // LANES * TILES
+
     def fetch_code(b):
-        at = pl.ds(b * chunk, chunk)
+        at = pl.ds(b * chunk // GROUP, chunk // GROUP)
         return pltpu.make_async_copy(c_ref.at[at], coded.at[at], sems.at[2, b])
 
     def fetch(b):
@@ -92,7 +101,7 @@
         at = pl.ds(b * chunk, chunk)
         return pltpu.make_async_copy(passages.at[at], p_ref.at[at], sems.at[1, b])
 
-    side = pltpu.make_async_copy(c_ref.at[:, pl.ds(width, LANES)], spares, sems.at[3, 2])
+    side = pltpu.make_async_copy(c_ref.at[:, slabs], spares, sems.at[3, 2])
     side.start()
     for b in range(NB):
         fetch_code(b).start()
@@ -102,7 +111,7 @@
     lower = at_ref[2] < LANES // 2
     side.wait()
     for z in range(NZ):
-        spare = spares[z * GROUP : z * GROUP + PBLK, :].astype(jnp.int32)
+        spare = spares[z].astype(jnp.int32)
         picks[z : z + 1, :] = jnp.where(lower, spare[:1], spare[1:2])
     picks[...] = pltpu.roll(picks[...], LANES - first, 1)
     local = pltpu.make_async_copy(picks, picked, sems.at[3, 0])
@@ -111,12 +120,18 @@
     tell.start()
     for b in range(NB):
         fetch_code(b).wait()
-        at = pl.ds(b * chunk, chunk)
-        code = coded[at]
-        shift = code[:, width:][:, LANES - 1 :].astype(jnp.float32)
-        half = jnp.floor(shift * 0.5)
-        low, high = jnp.exp2(half - shift), jnp.exp2(-half)
-        passages[at] = (code[:, :width].astype(jnp.float32) * low * high).astype(jnp.bfloat16)
+        for z in range(b * chunk // GROUP, (b + 1) * chunk // GROUP):
+            spare = spares[z].astype(jnp.float32)
+            columns = [spare[:, LANES - TILES + j :][:, :1] for j in range(TILES)]
+            shift = jnp.concatenate(columns, axis=0)
+            half = jnp.floor(shift * 0.5)
+            low, high = jnp.exp2(half - shift), jnp.exp2(-half)
+            for t in range(width // LANES):
+                value = coded[z, t * TILES : (t + 1) * TILES].astype(jnp.float32)
+                value = value.reshape(GROUP, LANES) * low * high
+                passages[z * GROUP : (z + 1) * GROUP, t * LANES : (t + 1) * LANES] = value.astype(
+                    jnp.bfloat16
+                )
         keep(b).start()
     local.wait()
 
@@ -148,11 +163,11 @@
         in_specs=[pl.BlockSpec(memory_space=pltpu.SMEM), apart, apart],
         out_specs=(pl.BlockSpec(memory_space=pltpu.VMEM), apart, apart),
         scratch_shapes=[
-            pltpu.VMEM((NZ * GROUP, width + LANES), jnp.bfloat16),
+            pltpu.VMEM((NZ, width // LANES * TILES + 1, PBLK, LANES), jnp.bfloat16),
             pltpu.VMEM((NB, QBLK, width), jnp.bfloat16),
             pltpu.VMEM((NZ * GROUP, width), jnp.bfloat16),
             pltpu.VMEM((CAND, width), jnp.bfloat16),
-            pltpu.VMEM((NZ * GROUP, LANES), jnp.bfloat16),
+            pltpu.VMEM((NZ, PBLK, LANES), jnp.bfloat16),
             pltpu.VMEM((NZ, LANES), jnp.int32),
             pltpu.SMEM((NZ, LANES), jnp.int32),
             pltpu.SemaphoreType.DMA((4, NB)),
@@ -227,19 +242,22 @@
     row = lax.broadcasted_iota(jnp.int32, (LANES, SHARE), 0)
     turned = jnp.where(row == 0, top, jnp.where(row == 1, total, 0.0)).T
     probs = jnp.exp(s_ref[...] - turned[:, :1]) / turned[:, 1:2]
-    w_ref[:SHARE] = (probs - hit_ref[...]).astype(jnp.bfloat16)
+    weights = (probs - hit_ref[...]).astype(jnp.bfloat16)
     loss = jnp.sum(losses, axis=1, keepdims=True)
     first = loss.astype(jnp.bfloat16).astype(jnp.float32)
     second = (loss - first).astype(jnp.bfloat16).astype(jnp.float32)
-    row = lax.broadcasted_iota(jnp.int32, (SENT - SHARE, CAND), 0)
+    row = lax.broadcasted_iota(jnp.int32, (SENT - SHARE, LANES), 0)
     pieces = jnp.where(row == 1, second, jnp.where(row == 2, loss - first - second, 0.0))
-    w_ref[SHARE:] = jnp.where(row == 0, first, pieces).astype(jnp.bfloat16)
+    pieces = jnp.where(row == 0, first, pieces).astype(jnp.bfloat16)
+    for h in range(HALVES):
+        w_ref[h, :SHARE] = weights[:, h * LANES : (h + 1) * LANES]
+        w_ref[h, SHARE:] = pieces
 
 
 def weigh(scores, hits, stats):
     return pl.pallas_call(
         weigh_kernel,
-        out_shape=jax.ShapeDtypeStruct((SENT, CAND), jnp.bfloat16),
+        out_shape=jax.ShapeDtypeStruct((HALVES, SENT, LANES), jnp.bfloat16),
         compiler_params=pltpu.CompilerParams(vmem_limit_bytes=8 << 20),
         cost_estimate=pl.CostEstimate(
             flops=10 * SHARE * CAND, bytes_accessed=6 * SHARE * CAND, transcendentals=SHARE * CAND
@@ -250,7 +268,8 @@
 
 def block_weights(w_ref, b):
     start = pl.multiple_of(lax.rem(b, PER_X) * QBLK, QBLK)
-    return w_ref[lax.div(b, PER_X), pl.ds(start, QBLK), :]
+    slab = lax.div(b, PER_X) * HALVES
+    return jnp.concatenate([w_ref[slab + h, pl.ds(start, QBLK), :] for h in range(HALVES)], axis=1)
 
 
 def passage_kernel(sel_ref, q_ref, w_ref, pg_ref, kept_ref, acc, sems):
@@ -260,9 +279,8 @@
     acc[...] = jnp.zeros_like(acc)
 
     def add(b, part, done):
-        rows = CAND // 2
         cand = lax.dot_general(
-            block_weights(w_ref, b)[:, part * rows : (part + 1) * rows],
+            w_ref[b // PER_X * HALVES + part, b % PER_X * QBLK : (b % PER_X + 1) * QBLK],
             q_ref[b][:, :width],
             (((0,), (0,)), ((), ())),
             preferred_element_type=jnp.float32,
@@ -279,8 +297,8 @@
 
     for part in range(2):
         for b in range(NB - 1):
-            add(jnp.int32(b), part, lambda z: None)
-        add(jnp.int32(NB - 1), part, lambda z: send(z).start())
+            add(b, part, lambda z: None)
+        add(NB - 1, part, lambda z: send(z).start())
     for z in range(NZ):
         send(z).wait()
     keep.wait()
@@ -335,7 +353,7 @@
             grid=(NY,),
             in_specs=[
                 pl.BlockSpec((NZ * GROUP, width), lambda k, sel, tab: (0, 0)),
-                pl.BlockSpec((NX, SENT, CAND), lambda k, sel, tab: (0, 0, 0)),
+                pl.BlockSpec((NX * HALVES, SENT, LANES), lambda k, sel, tab: (0, 0, 0)),
             ]
             + [block] * len(arrived),
             out_specs=block,
@@ -363,14 +381,15 @@
     code, marked = encode(passages, pair_block, queries, positives)
     q_all = lax.all_gather(marked, COL, axis=0, tiled=False)
     coded = lax.all_gather(code, "z", axis=0, tiled=True).astype(jnp.bfloat16)
+    coded = coded.reshape(NZ, *code.shape)
     part, p_all, sel = partial_scores(at, q_all, coded)
     parts = lax.all_to_all(
         part.reshape(NX, SHARE, CAND), "x", split_axis=0, concat_axis=0, tiled=True
     )
     scores, hits, stats = column_stats(at, parts, q_all)
     stats = lax.all_to_all(stats, COL, split_axis=0, concat_axis=0, tiled=True)
-    weights = lax.all_gather(weigh(scores, hits, stats), "x", axis=0, tiled=False)
-    loss = jnp.sum(weights[:, SHARE : SHARE + 3, :1].astype(jnp.float32))
+    weights = lax.all_gather(weigh(scores, hits, stats), "x", axis=0, tiled=True)
+    loss = jnp.sum(weights[::HALVES, SHARE : SHARE + 3, :1].astype(jnp.float32))
 
     passages_part, weights = passage_part(sel, q_all, weights)
     passage_grad = lax.psum_scatter(passages_part, "z", scatter_dimension=0, tiled=True)

time: 203 us -> 202 us (level)
  the two profiles are of different devices: /device:TPU:4 before, /device:TPU:2 now
where the time goes in v4:
time: 202 us
  blocking collectives  92.1 us (46%)
  waiting for transfers between devices  49.2 us (24%)
  Pallas kernels  26.3 us (13%)
  between operations  15.9 us (8%)
  starting transfers between devices  12.8 us (6%)
  other arithmetic  3.68 us (2%)
    all_gather x1, blocking collectives, per_device(): coded = lax.all_gather(code, 'z', axis=0, tiled=True).astype(jnp.bfloat16)  50.3 us
    all_to_all x1, waiting for transfers between devices, per_device(): lax.all_to_all(query_part(sel, mine, p_all, weights, arrived), 'y', split...  35.2 us
    all_to_all x1, blocking collectives, per_device(): lax.all_to_all(part.reshape(NX, SHARE, CAND), 'x', split_axis=0, concat_a...  18.6 us
    all_gather x1, blocking collectives, per_device(): lax.all_gather(weigh(scores, hits, stats), 'x', axis=0, tiled=True)  13 us
    pallas_call x2, Pallas kernels, query_part(): pl.pallas_call(query_kernel, out_shape=jax.ShapeDtypeStruct((NY, QBLK, wi...  11.4 us
    all_to_all x1, blocking collectives, per_device(): stats = lax.all_to_all(stats, COL, split_axis=0, concat_axis=0, tiled=True)  10.1 us
    all_to_all x1, waiting for transfers between devices, total_over(): lax.all_to_all(copies, axis, split_axis=0, concat_axis=0, tiled=True)  7.26 us
    all_to_all x1, starting transfers between devices, total_over(): lax.all_to_all(copies, axis, split_axis=0, concat_axis=0, tiled=True)  7.07 us
  transfers between devices with their start and end apart: 5, of which 3 were waited for; matrix products, arithmetic and copies ran while one was open for 3% of the time, Pallas kernels for 6%

profile of v4, /device:TPU:2, one launch (start us, length us, event | category | flops | bytes accessed | tf_op | source)
XLA Modules:
  0.0 201.8 jit_solution(17119633416989493878)
XLA Ops:
  7.2 2.0 encode.1
  9.2 0.0 reduce-scatter.2.cloned.1.call-start
  9.3 50.3 %all-gather.5 = f16[528,16,128]{2,1,0:T(8,128)(2,1)S(1)} all-gather(f16[33,16,128]{2,1,0:T(8,128)(2,1)S(1)} %convert_element_type.9), channel_id=1, replica_groups=mesh['z'=16,'y'=4,'core'=2,'x'=4] {'z'}, dimensions={0}, use_global_device_ids=true | all-gather | bytes 2297856 | tf_op jit(solution)/shard_map/all_gather | solution.py:383
  59.6 1.7 convert_element_type.10
  61.4 0.1 pad_add_fusion.at_ref
  61.5 6.4 %partial_scores.1 = (f32[1536,256]{1,0:T(8,128)S(1)}, bf16[1024,1024]{1,0:T(8,128)(2,1)}, s32[16,128]{1,0:T(8,128)}) custom-call(s32[3]{0:T(128)S(1)} %pad_add_fusion.at_ref, bf16[8,192,1152]{2,1,0:T(8,128)(2,1)} %bitcast.9, bf16[16,33,16,128]{3,2,1,0:T(8,128)(2,1)} %bitcast.13), custom_call_target="tpu_custom_call" | custom-call | flops 805306368 | bytes 8912896 | tf_op jit(solution)/shard_map/partial_scores/pallas_call | solution.py:156
  67.8 18.6 %all_to_all.20.part_ref = f32[4,384,256]{2,1,0:T(8,128)S(1)} all-to-all(f32[4,384,256]{2,1,0:T(8,128)S(1)} %bitcast.12), channel_id=1, replica_groups=mesh['z'=16,'y'=4,'core'=2,'x'=4] {'x'}, dimensions={0} | all-to-all | bytes 3145728 | tf_op jit(solution)/shard_map/all_to_all | solution.py:386
  86.5 2.3 %column_stats.1 = (f32[384,256]{1,0:T(8,128)S(1)}, f32[384,256]{1,0:T(8,128)S(1)}, f32[8,8,384]{2,1,0:T(8,128)S(1)}) custom-call(s32[3]{0:T(128)S(1)} %pad_add_fusion.at_ref, f32[4,384,256]{2,1,0:T(8,128)S(1)} %all_to_all.20.part_ref, bf16[8,192,1152]{2,1,0:T(8,128)(2,1)} %bitcast.10), custom_call_target="tpu_custom_call" | custom-call | flops 1179648 | bytes 1966080 | tf_op jit(solution)/shard_map/column_stats/pallas_call | solution.py:213
  88.7 10.1 %all_to_all.21.stat_ref = f32[8,8,384]{2,1,0:T(8,128)S(1)} all-to-all(f32[8,8,384]{2,1,0:T(8,128)S(1)} %get-tuple-element.18), channel_id=1, replica_groups=mesh['z'=16,'y'=4,'core'=2,'x'=4] {'y','core'}, dimensions={0} | all-to-all | bytes 196608 | tf_op jit(solution)/shard_map/all_to_all | solution.py:390
  98.9 0.4 weigh.1
  99.3 13.0 %all_gather.15.w_ref = bf16[8,400,128]{2,1,0:T(8,128)(2,1)S(1)} all-gather(bf16[2,400,128]{2,1,0:T(8,128)(2,1)S(1)} %weigh.1), channel_id=1, replica_groups=mesh['z'=16,'y'=4,'core'=2,'x'=4] {'x'}, dimensions={0}, use_global_device_ids=true | all-gather | bytes 1024000 | tf_op jit(solution)/shard_map/all_gather | solution.py:391
  112.3 3.9 %passage_part.1 = (f32[1024,1024]{1,0:T(8,128)}, bf16[8,400,128]{2,1,0:T(8,128)(2,1)}) custom-call(s32[16,128]{1,0:T(8,128)S(1)} %copy-done.1, bf16[8,192,1152]{2,1,0:T(8,128)(2,1)S(1)} %bitcast.11, bf16[8,400,128]{2,1,0:T(8,128)(2,1)S(1)} %all_gather.15.w_ref), custom_call_target="tpu_custom_call" | custom-call | flops 805306368 | bytes 8126464 | tf_op jit(solution)/shard_map/passage_part/pallas_call | solution.py:311
  116.3 5.2 %query_part.2 = f32[4,192,1024]{2,1,0:T(8,128)} custom-call(s32[16,128]{1,0:T(8,128)S(1)} %copy-done.1, s32[4]{0:T(128)S(1)} %fusion.tab_ref, bf16[1024,1024]{1,0:T(8,128)(2,1)} %get-tuple-element.20.p_ref, bf16[8,400,128]{2,1,0:T(8,128)(2,1)} %get-tuple-element.21.w_ref), custom_call_target="tpu_custom_call" | custom-call | flops 402653184 | bytes 6029312 | tf_op jit(solution)/shard_map/query_part/pallas_call | solution.py:348
  121.4 1.9 collective-permute-start
  123.3 0.6 convert_reduce_fusion
  123.9 1.3 broadcast_in_dim_broadcast_in_dim_broadcast_in_dim.3
  125.2 7.1 %all-to-all-start.2 = ((f32[16,8,128]{2,1,0:T(8,128)}), f32[16,8,128]{2,1,0:T(8,128)S(1)}, u32[]{:S(2)}, u32[]{:S(2)}) async-start(f32[16,8,128]{2,1,0:T(8,128)} %broadcast_in_dim_broadcast_in_dim_broadcast_in_dim.3), calls=%async_computation.2 | async-start | bytes 131072 | tf_op jit(solution)/shard_map/all_to_all | solution.py:374
  132.3 6.2 %query_part.3 = f32[4,192,1024]{2,1,0:T(8,128)} custom-call(s32[16,128]{1,0:T(8,128)S(1)} %copy-done.1, s32[4]{0:T(128)S(1)} %fusion.1.tab_ref, bf16[1024,1024]{1,0:T(8,128)(2,1)} %get-tuple-element.20.p_ref, bf16[8,400,128]{2,1,0:T(8,128)(2,1)} %get-tuple-element.21.w_ref, f32[4,192,1024]{2,1,0:T(8,128)} %collective-permute-done.rest_0_), custom_call_target="tpu_custom_call" | custom-call | flops 402653184 | bytes 6029312 | tf_op jit(solution)/shard_map/query_part/pallas_call | solution.py:348
  138.6 7.3 %all-to-all-done.2 = f32[16,8,128]{2,1,0:T(8,128)S(1)} async-done(((f32[16,8,128]{2,1,0:T(8,128)}), f32[16,8,128]{2,1,0:T(8,128)S(1)}, u32[]{:S(2)}, u32[]{:S(2)}) %all-to-all-start.2) | async-done | bytes 65568 | tf_op jit(solution)/shard_map/all_to_all | solution.py:374
  145.8 3.7 %all-to-all-start.3 = ((f32[4,192,1024]{2,1,0:T(8,128)}), f32[4,192,1024]{2,1,0:T(8,128)S(1)}, u32[]{:S(2)}, u32[]{:S(2)}) async-start(f32[4,192,1024]{2,1,0:T(8,128)} %query_part.3), calls=%async_computation.3 | async-start | bytes 6291456 | tf_op jit(solution)/shard_map/all_to_all | solution.py:400
  149.6 0.5 slice.7
  150.7 35.2 %all-to-all-done.3 = f32[4,192,1024]{2,1,0:T(8,128)S(1)} async-done(((f32[4,192,1024]{2,1,0:T(8,128)}), f32[4,192,1024]{2,1,0:T(8,128)S(1)}, u32[]{:S(2)}, u32[]{:S(2)}) %all-to-all-start.3) | async-done | bytes 3145760 | tf_op jit(solution)/shard_map/all_to_all | solution.py:400
  185.9 1.2 reduce_sum.29
  187.1 6.6 %reduce-scatter.2.cloned.1.call-done = f32[64,1024]{1,0:T(8,128)} async-done(((f32[1024,1024]{1,0:T(8,128)}), f32[64,1024]{1,0:T(8,128)}) %reduce-scatter.2.cloned.1.call-update) | async-done | bytes 262160 | tf_op jit(solution)/shard_map/reduce_scatter | solution.py:395
  (13 shorter events, 0.1 us)
Async XLA Ops:
  7.2 54.3 %all-gather.4.cloned.1.call-start = ((), (), s32[]{:S(2)}) async-start(), calls=%async_computation.6 | async-start | bytes 3981312 | tf_op jit(solution)/shard_map/all_gather | solution.py:382
  9.2 184.6 %reduce-scatter.2.cloned.1.call-start = ((), (), s32[]{:S(2)}) async-start(), calls=%async_computation.5 | async-start | bytes 4456448 | tf_op jit(solution)/shard_map/reduce_scatter | solution.py:395
  86.5 25.8 %copy-start = (bf16[1536,1152]{1,0:T(8,128)(2,1)S(1)}, bf16[1536,1152]{1,0:T(8,128)(2,1)}, u32[]{:S(2)}) copy-start(bf16[1536,1152]{1,0:T(8,128)(2,1)} %all-gather.4.cloned.1.call-done) | copy-start | bytes 10616836
  86.5 25.8 %copy-start.1 = (s32[16,128]{1,0:T(8,128)S(1)}, s32[16,128]{1,0:T(8,128)}, u32[]{:S(2)}) copy-start(s32[16,128]{1,0:T(8,128)} %get-tuple-element.19.sel_ref) | copy-start | bytes 24580
  121.4 10.9 %collective-permute-start = (f32[4,192,1024]{2,1,0:T(8,128)}, f32[4,192,1024]{2,1,0:T(8,128)}, u32[]{:S(2)}, u32[]{:S(2)}) collective-permute-start(f32[4,192,1024]{2,1,0:T(8,128)} %query_part.2), channel_id=1, source_target_pairs={{0,4},{4,0},{1,5},{5,1},{2,6},{6,2},{3,7},{7,3},{8,12},{12,8},{9,1... | collective-permute-start | bytes 9437192 | tf_op jit(solution)/shard_map/ppermute | solution.py:398
  125.2 20.6 %all-to-all-start.2 = ((f32[16,8,128]{2,1,0:T(8,128)}), f32[16,8,128]{2,1,0:T(8,128)S(1)}, u32[]{:S(2)}, u32[]{:S(2)}) async-start(f32[16,8,128]{2,1,0:T(8,128)} %broadcast_in_dim_broadcast_in_dim_broadcast_in_dim.3), calls=%async_computation.2 | async-start | bytes 131072 | tf_op jit(solution)/shard_map/all_to_all | solution.py:374
  145.8 40.1 %all-to-all-start.3 = ((f32[4,192,1024]{2,1,0:T(8,128)}), f32[4,192,1024]{2,1,0:T(8,128)S(1)}, u32[]{:S(2)}, u32[]{:S(2)}) async-start(f32[4,192,1024]{2,1,0:T(8,128)} %query_part.3), calls=%async_computation.3 | async-start | bytes 6291456 | tf_op jit(solution)/shard_map/all_to_all | solution.py:400
Sparse Core Ops, SparseCore 0:
  10.7 41.5 all-gather.3
  116.4 77.3 reduce-scatter.1

commit v5 on v4

--- a/solution.py
+++ b/solution.py
@@ -90,6 +90,9 @@
 
     slabs = width // LANES * TILES
 
+    def exponents(tile):
+        return jnp.concatenate([tile[:, LANES - TILES + j :][:, :1] for j in range(TILES)], axis=0)
+
     def fetch_code(b):
         at = pl.ds(b * chunk // GROUP, chunk // GROUP)
         return pltpu.make_async_copy(c_ref.at[at], coded.at[at], sems.at[2, b])
@@ -121,11 +124,9 @@
     for b in range(NB):
         fetch_code(b).wait()
         for z in range(b * chunk // GROUP, (b + 1) * chunk // GROUP):
-            spare = spares[z].astype(jnp.float32)
-            columns = [spare[:, LANES - TILES + j :][:, :1] for j in range(TILES)]
-            shift = jnp.concatenate(columns, axis=0)
+            shift = spares[z].astype(jnp.float32)
             half = jnp.floor(shift * 0.5)
-            low, high = jnp.exp2(half - shift), jnp.exp2(-half)
+            low, high = exponents(jnp.exp2(half - shift)), exponents(jnp.exp2(-half))
             for t in range(width // LANES):
                 value = coded[z, t * TILES : (t + 1) * TILES].astype(jnp.float32)
                 value = value.reshape(GROUP, LANES) * low * high

time: 202 us -> 202 us (level)
  the two profiles are of different devices: /device:TPU:2 before, /device:TPU:4 now
where the time goes in v5:
time: 202 us
  blocking collectives  92.5 us (46%)
  waiting for transfers between devices  48.8 us (24%)
  Pallas kernels  26.3 us (13%)
  between operations  15.9 us (8%)
  starting transfers between devices  12.8 us (6%)
  other arithmetic  3.68 us (2%)
    all_gather x1, blocking collectives, per_device(): coded = lax.all_gather(code, 'z', axis=0, tiled=True).astype(jnp.bfloat16)  50.3 us
    all_to_all x1, waiting for transfers between devices, per_device(): lax.all_to_all(query_part(sel, mine, p_all, weights, arrived), 'y', split...  35.2 us
    all_to_all x1, blocking collectives, per_device(): lax.all_to_all(part.reshape(NX, SHARE, CAND), 'x', split_axis=0, concat_a...  17.4 us
    all_gather x1, blocking collectives, per_device(): lax.all_gather(weigh(scores, hits, stats), 'x', axis=0, tiled=True)  14.7 us
    pallas_call x2, Pallas kernels, query_part(): pl.pallas_call(query_kernel, out_shape=jax.ShapeDtypeStruct((NY, QBLK, wi...  11.4 us
    all_to_all x1, blocking collectives, per_device(): stats = lax.all_to_all(stats, COL, split_axis=0, concat_axis=0, tiled=True)  10.1 us
    all_to_all x1, waiting for transfers between devices, total_over(): lax.all_to_all(copies, axis, split_axis=0, concat_axis=0, tiled=True)  7.22 us
    all_to_all x1, starting transfers between devices, total_over(): lax.all_to_all(copies, axis, split_axis=0, concat_axis=0, tiled=True)  7.09 us
  transfers between devices with their start and end apart: 5, of which 3 were waited for; matrix products, arithmetic and copies ran while one was open for 3% of the time, Pallas kernels for 6%

profile of v5, /device:TPU:4, one launch (start us, length us, event | category | flops | bytes accessed | tf_op | source)
XLA Modules:
  0.0 201.8 jit_solution(15456513379153687627)
XLA Ops:
  7.2 2.0 encode.1
  9.2 0.0 reduce-scatter.2.cloned.1.call-start
  9.3 50.3 %all-gather.5 = f16[528,16,128]{2,1,0:T(8,128)(2,1)S(1)} all-gather(f16[33,16,128]{2,1,0:T(8,128)(2,1)S(1)} %convert_element_type.9), channel_id=1, replica_groups=mesh['z'=16,'y'=4,'core'=2,'x'=4] {'z'}, dimensions={0}, use_global_device_ids=true | all-gather | bytes 2297856 | tf_op jit(solution)/shard_map/all_gather | solution.py:384
  59.6 1.7 convert_element_type.10
  61.4 0.1 pad_add_fusion.at_ref
  61.5 6.3 %partial_scores.1 = (f32[1536,256]{1,0:T(8,128)S(1)}, bf16[1024,1024]{1,0:T(8,128)(2,1)}, s32[16,128]{1,0:T(8,128)}) custom-call(s32[3]{0:T(128)S(1)} %pad_add_fusion.at_ref, bf16[8,192,1152]{2,1,0:T(8,128)(2,1)} %bitcast.9, bf16[16,33,16,128]{3,2,1,0:T(8,128)(2,1)} %bitcast.13), custom_call_target="tpu_custom_call" | custom-call | flops 805306368 | bytes 8912896 | tf_op jit(solution)/shard_map/partial_scores/pallas_call | solution.py:157
  67.8 17.4 %all_to_all.20.part_ref = f32[4,384,256]{2,1,0:T(8,128)S(1)} all-to-all(f32[4,384,256]{2,1,0:T(8,128)S(1)} %bitcast.12), channel_id=1, replica_groups=mesh['z'=16,'y'=4,'core'=2,'x'=4] {'x'}, dimensions={0} | all-to-all | bytes 3145728 | tf_op jit(solution)/shard_map/all_to_all | solution.py:387
  85.2 2.3 %column_stats.1 = (f32[384,256]{1,0:T(8,128)S(1)}, f32[384,256]{1,0:T(8,128)S(1)}, f32[8,8,384]{2,1,0:T(8,128)S(1)}) custom-call(s32[3]{0:T(128)S(1)} %pad_add_fusion.at_ref, f32[4,384,256]{2,1,0:T(8,128)S(1)} %all_to_all.20.part_ref, bf16[8,192,1152]{2,1,0:T(8,128)(2,1)} %bitcast.10), custom_call_target="tpu_custom_call" | custom-call | flops 1179648 | bytes 1966080 | tf_op jit(solution)/shard_map/column_stats/pallas_call | solution.py:214
  87.4 10.1 %all_to_all.21.stat_ref = f32[8,8,384]{2,1,0:T(8,128)S(1)} all-to-all(f32[8,8,384]{2,1,0:T(8,128)S(1)} %get-tuple-element.18), channel_id=1, replica_groups=mesh['z'=16,'y'=4,'core'=2,'x'=4] {'y','core'}, dimensions={0} | all-to-all | bytes 196608 | tf_op jit(solution)/shard_map/all_to_all | solution.py:391
  97.6 0.4 weigh.1
  98.0 14.7 %all_gather.15.w_ref = bf16[8,400,128]{2,1,0:T(8,128)(2,1)S(1)} all-gather(bf16[2,400,128]{2,1,0:T(8,128)(2,1)S(1)} %weigh.1), channel_id=1, replica_groups=mesh['z'=16,'y'=4,'core'=2,'x'=4] {'x'}, dimensions={0}, use_global_device_ids=true | all-gather | bytes 1024000 | tf_op jit(solution)/shard_map/all_gather | solution.py:392
  112.7 3.9 %passage_part.1 = (f32[1024,1024]{1,0:T(8,128)}, bf16[8,400,128]{2,1,0:T(8,128)(2,1)}) custom-call(s32[16,128]{1,0:T(8,128)S(1)} %copy-done.1, bf16[8,192,1152]{2,1,0:T(8,128)(2,1)S(1)} %bitcast.11, bf16[8,400,128]{2,1,0:T(8,128)(2,1)S(1)} %all_gather.15.w_ref), custom_call_target="tpu_custom_call" | custom-call | flops 805306368 | bytes 8126464 | tf_op jit(solution)/shard_map/passage_part/pallas_call | solution.py:312
  116.6 5.2 %query_part.2 = f32[4,192,1024]{2,1,0:T(8,128)} custom-call(s32[16,128]{1,0:T(8,128)S(1)} %copy-done.1, s32[4]{0:T(128)S(1)} %fusion.tab_ref, bf16[1024,1024]{1,0:T(8,128)(2,1)} %get-tuple-element.20.p_ref, bf16[8,400,128]{2,1,0:T(8,128)(2,1)} %get-tuple-element.21.w_ref), custom_call_target="tpu_custom_call" | custom-call | flops 402653184 | bytes 6029312 | tf_op jit(solution)/shard_map/query_part/pallas_call | solution.py:349
  121.8 1.9 collective-permute-start
  123.7 0.6 convert_reduce_fusion
  124.3 1.3 broadcast_in_dim_broadcast_in_dim_broadcast_in_dim.3
  125.6 7.1 %all-to-all-start.2 = ((f32[16,8,128]{2,1,0:T(8,128)}), f32[16,8,128]{2,1,0:T(8,128)S(1)}, u32[]{:S(2)}, u32[]{:S(2)}) async-start(f32[16,8,128]{2,1,0:T(8,128)} %broadcast_in_dim_broadcast_in_dim_broadcast_in_dim.3), calls=%async_computation.2 | async-start | bytes 131072 | tf_op jit(solution)/shard_map/all_to_all | solution.py:375
  132.7 6.3 %query_part.3 = f32[4,192,1024]{2,1,0:T(8,128)} custom-call(s32[16,128]{1,0:T(8,128)S(1)} %copy-done.1, s32[4]{0:T(128)S(1)} %fusion.1.tab_ref, bf16[1024,1024]{1,0:T(8,128)(2,1)} %get-tuple-element.20.p_ref, bf16[8,400,128]{2,1,0:T(8,128)(2,1)} %get-tuple-element.21.w_ref, f32[4,192,1024]{2,1,0:T(8,128)} %collective-permute-done.rest_0_), custom_call_target="tpu_custom_call" | custom-call | flops 402653184 | bytes 6029312 | tf_op jit(solution)/shard_map/query_part/pallas_call | solution.py:349
  138.9 7.2 %all-to-all-done.2 = f32[16,8,128]{2,1,0:T(8,128)S(1)} async-done(((f32[16,8,128]{2,1,0:T(8,128)}), f32[16,8,128]{2,1,0:T(8,128)S(1)}, u32[]{:S(2)}, u32[]{:S(2)}) %all-to-all-start.2) | async-done | bytes 65568 | tf_op jit(solution)/shard_map/all_to_all | solution.py:375
  146.2 3.7 %all-to-all-start.3 = ((f32[4,192,1024]{2,1,0:T(8,128)}), f32[4,192,1024]{2,1,0:T(8,128)S(1)}, u32[]{:S(2)}, u32[]{:S(2)}) async-start(f32[4,192,1024]{2,1,0:T(8,128)} %query_part.3), calls=%async_computation.3 | async-start | bytes 6291456 | tf_op jit(solution)/shard_map/all_to_all | solution.py:401
  149.9 0.5 slice.7
  151.1 35.2 %all-to-all-done.3 = f32[4,192,1024]{2,1,0:T(8,128)S(1)} async-done(((f32[4,192,1024]{2,1,0:T(8,128)}), f32[4,192,1024]{2,1,0:T(8,128)S(1)}, u32[]{:S(2)}, u32[]{:S(2)}) %all-to-all-start.3) | async-done | bytes 3145760 | tf_op jit(solution)/shard_map/all_to_all | solution.py:401
  186.3 1.2 reduce_sum.29
  187.5 6.4 %reduce-scatter.2.cloned.1.call-done = f32[64,1024]{1,0:T(8,128)} async-done(((f32[1024,1024]{1,0:T(8,128)}), f32[64,1024]{1,0:T(8,128)}) %reduce-scatter.2.cloned.1.call-update) | async-done | bytes 262160 | tf_op jit(solution)/shard_map/reduce_scatter | solution.py:396
  (13 shorter events, 0.1 us)
Async XLA Ops:
  7.2 54.3 %all-gather.4.cloned.1.call-start = ((), (), s32[]{:S(2)}) async-start(), calls=%async_computation.6 | async-start | bytes 3981312 | tf_op jit(solution)/shard_map/all_gather | solution.py:383
  9.2 184.6 %reduce-scatter.2.cloned.1.call-start = ((), (), s32[]{:S(2)}) async-start(), calls=%async_computation.5 | async-start | bytes 4456448 | tf_op jit(solution)/shard_map/reduce_scatter | solution.py:396
  85.2 27.5 %copy-start = (bf16[1536,1152]{1,0:T(8,128)(2,1)S(1)}, bf16[1536,1152]{1,0:T(8,128)(2,1)}, u32[]{:S(2)}) copy-start(bf16[1536,1152]{1,0:T(8,128)(2,1)} %all-gather.4.cloned.1.call-done) | copy-start | bytes 10616836
  85.2 27.5 %copy-start.1 = (s32[16,128]{1,0:T(8,128)S(1)}, s32[16,128]{1,0:T(8,128)}, u32[]{:S(2)}) copy-start(s32[16,128]{1,0:T(8,128)} %get-tuple-element.19.sel_ref) | copy-start | bytes 24580
  121.8 10.9 %collective-permute-start = (f32[4,192,1024]{2,1,0:T(8,128)}, f32[4,192,1024]{2,1,0:T(8,128)}, u32[]{:S(2)}, u32[]{:S(2)}) collective-permute-start(f32[4,192,1024]{2,1,0:T(8,128)} %query_part.2), channel_id=1, source_target_pairs={{0,4},{4,0},{1,5},{5,1},{2,6},{6,2},{3,7},{7,3},{8,12},{12,8},{9,1... | collective-permute-start | bytes 9437192 | tf_op jit(solution)/shard_map/ppermute | solution.py:399
  125.6 20.6 %all-to-all-start.2 = ((f32[16,8,128]{2,1,0:T(8,128)}), f32[16,8,128]{2,1,0:T(8,128)S(1)}, u32[]{:S(2)}, u32[]{:S(2)}) async-start(f32[16,8,128]{2,1,0:T(8,128)} %broadcast_in_dim_broadcast_in_dim_broadcast_in_dim.3), calls=%async_computation.2 | async-start | bytes 131072 | tf_op jit(solution)/shard_map/all_to_all | solution.py:375
  146.2 40.1 %all-to-all-start.3 = ((f32[4,192,1024]{2,1,0:T(8,128)}), f32[4,192,1024]{2,1,0:T(8,128)S(1)}, u32[]{:S(2)}, u32[]{:S(2)}) async-start(f32[4,192,1024]{2,1,0:T(8,128)} %query_part.3), calls=%async_computation.3 | async-start | bytes 6291456 | tf_op jit(solution)/shard_map/all_to_all | solution.py:401
Sparse Core Ops, SparseCore 0:
  10.7 41.5 all-gather.3
  116.7 77.0 reduce-scatter.1
